TPU v7x, 128 devices: a whole 4x4x4 slice. The times are simulated.
128 devices in a mesh: dp: 16 (over x, y_hi, core), tensor: 8 (over z, y_lo).
Axes of the slice: x: 4, y: 4 (y_hi: 2, y_lo: 2; y = y_hi * 2 + y_lo), z: 4, core: 2. Of those that a mesh axis runs over, the one named last changes fastest.
Arguments:
- tokens: bfloat16 [16, 2, 512, 2048], P('dp', None, 'tensor'), may hold values from -6 to 6
- lengths: int32 [16, 2], P('dp'), may hold values from 128 to 512, as said below
- cotangent: bfloat16 [16, 2, 512, 2048], P('dp', None, 'tensor'), may hold values from -6 to 6
- attn_gain: float32 [2048], replicated, may hold values from 0.1 to 1.9
- mixer_in: bfloat16 [2048, 4, 2048], P(None, None, 'tensor'), may hold values from -0.125 to 0.125
- rate_proj: bfloat16 [2048, 2, 16], P(None, None, 'tensor'), may hold values from -0.125 to 0.125
- conv_weight: float32 [3, 4, 2048], P(None, None, 'tensor'), may hold values from -2.5 to 2.5
- decay_rate: float32 [16], P('tensor'), may hold values from 0.05 to 4
- decay_bias: float32 [16], P('tensor'), may hold values from -5 to -2
- out_gain: float32 [128], replicated, may hold values from 0.25 to 1.75
- out_proj: bfloat16 [2048, 2048], P('tensor'), may hold values from -0.25 to 0.25
- ffn_gain: float32 [2048], replicated, may hold values from 0.1 to 1.9
- gate_up: bfloat16 [2048, 2, 5632], P(None, None, 'tensor'), may hold values from -0.125 to 0.125
- down_proj: bfloat16 [5632, 2048], P('tensor'), may hold values from -0.109375 to 0.109375
Outputs:
- layer_out: bfloat16 [16, 2, 512, 2048], P('dp', None, 'tensor')
- d_tokens: bfloat16 [16, 2, 512, 2048], P('dp', None, 'tensor')
- d_attn_gain: float32 [2048], replicated
- d_mixer_in: float32 [2048, 4, 2048], P(None, None, 'tensor')
- d_rate_proj: float32 [2048, 2, 16], P(None, None, 'tensor')
- d_conv_weight: float32 [3, 4, 2048], P(None, None, 'tensor')
- d_decay_rate: float32 [16], P('tensor')
- d_decay_bias: float32 [16], P('tensor')
- d_out_gain: float32 [128], replicated
- d_out_proj: float32 [2048, 2048], P('tensor')
- d_ffn_gain: float32 [2048], replicated
- d_gate_up: float32 [2048, 2, 5632], P(None, None, 'tensor')
- d_down_proj: float32 [5632, 2048], P('tensor')
Inputs may be any that keep to these rules, and one draw needn't show every extreme that they name: `lengths`: in each group at least one microbatch has all 512 tokens live; positions at or past a microbatch's length are padding.
All inputs are finite; a program needn't handle non-finite values.
Results may differ from a plain program's by a relative error of at most 0.04.
Values may be sent and summed in bfloat16 or wider, within the bound.
No kernel may reach another device: no remote copies, remote signals or barrier semaphores. Data moves between devices by JAX's collectives and lax.ppermute only.
A program may use at most 320 MiB of HBM per device.

v0:
```python
import jax
import jax.numpy as jnp
from jax import lax
from jax.sharding import PartitionSpec as P

BLOCK = 64


EPS = 1e-06
HIGH = lax.Precision.HIGHEST


def unit_lower_inverse(lower):
    size = lower.shape[-1]
    if size == 1:
        return jnp.ones_like(lower)
    half = size // 2
    top = unit_lower_inverse(lower[..., :half, :half])
    bottom = unit_lower_inverse(lower[..., half:, half:])
    middle = jnp.einsum("...ij,...jk->...ik", lower[..., half:, :half], top, precision=HIGH)
    corner = -jnp.einsum("...ij,...jk->...ik", bottom, middle, precision=HIGH)
    upper_rows = jnp.concatenate(
        [top, jnp.zeros(top.shape[:-1] + (size - half,), lower.dtype)], axis=-1
    )
    lower_rows = jnp.concatenate([corner, bottom], axis=-1)
    return jnp.concatenate([upper_rows, lower_rows], axis=-2)


def state_step(carried, pieces):
    queries, solved_keys, solved_values, attend, decay_to, tail_keys, last_decay = pieces
    errors = solved_values - jnp.einsum("htd,hde->hte", solved_keys, carried, precision=HIGH)
    block_out = decay_to[..., None] * jnp.einsum("htd,hde->hte", queries, carried, precision=HIGH)
    block_out = block_out + jnp.einsum("htj,hje->hte", attend, errors, precision=HIGH)
    new_state = last_decay[:, None, None] * carried + jnp.einsum(
        "hjd,hje->hde", tail_keys, errors, precision=HIGH
    )
    return (new_state, block_out)


def mixer_core(projected, rates, conv_weight, decay_rate, decay_bias, out_gain):
    positions = projected.shape[0]
    head_count = rates.shape[2]
    head_size = projected.shape[2] // head_count
    kernel_taps = conv_weight.shape[1]
    padded = jnp.pad(projected[:, :3, :], ((kernel_taps - 1, 0), (0, 0), (0, 0)))
    conv_out = padded[0:positions] * conv_weight[:, 0, :]
    for offset in range(1, kernel_taps):
        conv_out = conv_out + padded[offset : offset + positions] * conv_weight[:, offset, :]
    conv_out = jax.nn.silu(conv_out).reshape(positions, 3, head_count, head_size)
    queries = conv_out[:, 0]
    key_rows = conv_out[:, 1]
    values = conv_out[:, 2]
    queries = (
        queries
        * lax.rsqrt(jnp.sum(queries * queries, -1, keepdims=True) + EPS)
        * head_size ** (-0.5)
    )
    key_rows = key_rows * lax.rsqrt(jnp.sum(key_rows * key_rows, -1, keepdims=True) + EPS)
    update_rate = jax.nn.sigmoid(rates[:, 1])
    logdecay = -decay_rate * jax.nn.softplus(rates[:, 0] + decay_bias)
    blocks = positions // BLOCK

    def arrange(array):
        return array.reshape(blocks, BLOCK, head_count, head_size).transpose(0, 2, 1, 3)

    def arrange_flat(array):
        return array.reshape(blocks, BLOCK, head_count).transpose(0, 2, 1)

    queries = arrange(queries)
    key_rows = arrange(key_rows)
    values = arrange(values)
    update_rate = arrange_flat(update_rate)
    cumul = jnp.cumsum(arrange_flat(logdecay), axis=2)
    row_index = jnp.arange(BLOCK)[:, None]
    col_index = jnp.arange(BLOCK)[None, :]
    lower_mask = row_index >= col_index
    strict_mask = row_index > col_index
    spread = cumul[..., :, None] - cumul[..., None, :]
    decay_ratio = jnp.where(lower_mask, jnp.exp(jnp.where(lower_mask, spread, 0.0)), 0.0)
    keys_keys = jnp.einsum("bhtd,bhjd->bhtj", key_rows, key_rows, precision=HIGH)
    system = jnp.where(
        strict_mask, decay_ratio * keys_keys * update_rate[..., None, :], 0.0
    ) + jnp.eye(BLOCK, dtype=keys_keys.dtype)
    inverse = unit_lower_inverse(system)
    decay_to = jnp.exp(cumul)
    solved_values = jnp.einsum("bhtj,bhjd->bhtd", inverse, values, precision=HIGH)
    solved_keys = jnp.einsum(
        "bhtj,bhjd->bhtd", inverse, decay_to[..., None] * key_rows, precision=HIGH
    )
    attend = (
        decay_ratio
        * jnp.einsum("bhtd,bhjd->bhtj", queries, key_rows, precision=HIGH)
        * update_rate[..., None, :]
    )
    tail_keys = key_rows * (jnp.exp(cumul[..., -1:] - cumul) * update_rate)[..., None]
    last_decay = jnp.exp(cumul[..., -1])
    start_state = jnp.zeros((head_count, head_size, head_size), projected.dtype)
    _, outputs = lax.scan(
        jax.checkpoint(state_step),
        start_state,
        (queries, solved_keys, solved_values, attend, decay_to, tail_keys, last_decay),
    )
    outputs = outputs.transpose(0, 2, 1, 3).reshape(positions, head_count, head_size)
    norm_scale = lax.rsqrt(jnp.mean(outputs * outputs, -1, keepdims=True) + EPS)
    out_gate = projected[:, 3].reshape(positions, head_count, head_size)
    return (outputs * norm_scale * out_gain * jax.nn.silu(out_gate)).reshape(
        positions, head_count * head_size
    )


def rows_product(matrix, weight):
    return jnp.dot(matrix, weight, preferred_element_type=jnp.float32)


def ffn_rows_back(d_both, gate_up):
    return jnp.einsum("lkf,dkf->ld", d_both, gate_up, preferred_element_type=jnp.float32)


def mixer_rows_back(d_proj, d_rates, mixer_in, rate_proj):
    first = jnp.einsum("lkf,dkf->ld", d_proj, mixer_in, preferred_element_type=jnp.float32)
    return first + jnp.einsum("lkh,dkh->ld", d_rates, rate_proj, preferred_element_type=jnp.float32)


def norm_back(values, norm_scale, gain, d_normed):
    weighted = d_normed * gain
    d_gain = jnp.sum(d_normed * values * norm_scale, 0)
    d_values = norm_scale * weighted - values * norm_scale**3 * jnp.mean(
        weighted * values, -1, keepdims=True
    )
    return (d_values, d_gain)


def shards(
    tokens,
    lengths,
    cotangent,
    attn_gain,
    mixer_in,
    rate_proj,
    conv_weight,
    decay_rate,
    decay_bias,
    out_gain,
    out_proj,
    ffn_gain,
    gate_up,
    down_proj,
):
    shard_rows = tokens.shape[2]
    micro_count = tokens.shape[1]
    places = lax.axis_index("tensor") * shard_rows + jnp.arange(shard_rows, dtype=jnp.int32)
    d_attn_gain = jnp.zeros(attn_gain.shape, jnp.float32)
    d_ffn_gain = jnp.zeros(ffn_gain.shape, jnp.float32)
    d_out_gain = jnp.zeros(out_gain.shape, jnp.float32)
    d_mixer_in = jnp.zeros(mixer_in.shape, jnp.float32)
    d_rate_proj = jnp.zeros(rate_proj.shape, jnp.float32)
    d_conv = jnp.zeros(conv_weight.shape, jnp.float32)
    d_decay = jnp.zeros(decay_rate.shape, jnp.float32)
    d_bias = jnp.zeros(decay_bias.shape, jnp.float32)
    d_out_proj = jnp.zeros(out_proj.shape, jnp.float32)
    d_gate_up = jnp.zeros(gate_up.shape, jnp.float32)
    d_down = jnp.zeros(down_proj.shape, jnp.float32)
    results = []
    input_grads = []
    for microbatch in range(micro_count):
        source = tokens[0, microbatch].astype(jnp.float32)
        valid = (places < lengths[0, microbatch]).astype(jnp.float32)[:, None]
        scale_one = lax.rsqrt(jnp.mean(source * source, -1, keepdims=True) + EPS)
        normed_one = (source * scale_one * attn_gain).astype(jnp.bfloat16)
        rows_one = lax.all_gather(normed_one, "tensor", axis=0, tiled=True)
        projected = jnp.einsum(
            "ld,dkf->lkf", rows_one, mixer_in, preferred_element_type=jnp.float32
        )
        rates = jnp.einsum("ld,dkh->lkh", rows_one, rate_proj, preferred_element_type=jnp.float32)
        core_out, core_back = jax.vjp(
            mixer_core, projected, rates, conv_weight, decay_rate, decay_bias, out_gain
        )
        mixer_rows = core_out.astype(jnp.bfloat16)
        attended = lax.psum_scatter(
            rows_product(mixer_rows, out_proj), "tensor", scatter_dimension=0, tiled=True
        )
        hidden = source + attended
        scale_two = lax.rsqrt(jnp.mean(hidden * hidden, -1, keepdims=True) + EPS)
        normed_two = (hidden * scale_two * ffn_gain).astype(jnp.bfloat16)
        rows_two = lax.all_gather(normed_two, "tensor", axis=0, tiled=True)
        both = jnp.einsum("ld,dkf->lkf", rows_two, gate_up, preferred_element_type=jnp.float32)
        gate_act = jax.nn.silu(both[:, 0])
        inner = (gate_act * both[:, 1]).astype(jnp.bfloat16)
        branch = lax.psum_scatter(
            rows_product(inner, down_proj).astype(jnp.bfloat16),
            "tensor",
            scatter_dimension=0,
            tiled=True,
        ).astype(jnp.float32)
        results.append(((hidden + branch) * valid).astype(jnp.bfloat16))
        grad_out = cotangent[0, microbatch].astype(jnp.float32) * valid
        grad_rows = lax.all_gather(grad_out.astype(jnp.bfloat16), "tensor", axis=0, tiled=True)
        d_down = d_down + lax.dot_general(
            inner, grad_rows, (((0,), (0,)), ((), ())), preferred_element_type=jnp.float32
        )
        d_inner = lax.dot_general(
            grad_rows, down_proj, (((1,), (1,)), ((), ())), preferred_element_type=jnp.float32
        )
        sigma = jax.nn.sigmoid(both[:, 0])
        d_gate = d_inner * both[:, 1] * sigma * (1.0 + both[:, 0] * (1.0 - sigma))
        d_both = jnp.stack([d_gate, d_inner * gate_act], axis=1).astype(jnp.bfloat16)
        d_gate_up = d_gate_up + jnp.einsum(
            "ld,lkf->dkf", rows_two, d_both, preferred_element_type=jnp.float32
        )
        d_normed_two = lax.psum_scatter(
            ffn_rows_back(d_both, gate_up).astype(jnp.bfloat16),
            "tensor",
            scatter_dimension=0,
            tiled=True,
        ).astype(jnp.float32)
        d_from_two, gain_part = norm_back(hidden, scale_two, ffn_gain, d_normed_two)
        d_ffn_gain = d_ffn_gain + gain_part
        d_hidden = grad_out + d_from_two
        grad_attn = lax.all_gather(d_hidden.astype(jnp.bfloat16), "tensor", axis=0, tiled=True)
        d_out_proj = d_out_proj + lax.dot_general(
            mixer_rows, grad_attn, (((0,), (0,)), ((), ())), preferred_element_type=jnp.float32
        )
        d_mixer_rows = lax.dot_general(
            grad_attn, out_proj, (((1,), (1,)), ((), ())), preferred_element_type=jnp.float32
        )
        d_proj, d_rates, conv_part, decay_part, bias_part, out_gain_part = core_back(d_mixer_rows)
        d_conv = d_conv + conv_part
        d_decay = d_decay + decay_part
        d_bias = d_bias + bias_part
        d_out_gain = d_out_gain + out_gain_part
        d_proj_low = d_proj.astype(jnp.bfloat16)
        d_rates_low = d_rates.astype(jnp.bfloat16)
        d_mixer_in = d_mixer_in + jnp.einsum(
            "ld,lkf->dkf", rows_one, d_proj_low, preferred_element_type=jnp.float32
        )
        d_rate_proj = d_rate_proj + jnp.einsum(
            "ld,lkh->dkh", rows_one, d_rates_low, preferred_element_type=jnp.float32
        )
        d_normed_one = lax.psum_scatter(
            mixer_rows_back(d_proj_low, d_rates_low, mixer_in, rate_proj).astype(jnp.bfloat16),
            "tensor",
            scatter_dimension=0,
            tiled=True,
        ).astype(jnp.float32)
        d_from_one, gain_first = norm_back(source, scale_one, attn_gain, d_normed_one)
        d_attn_gain = d_attn_gain + gain_first
        input_grads.append((d_hidden + d_from_one).astype(jnp.bfloat16))
    d_mixer_in, d_rate_proj, d_conv, d_decay, d_bias, d_out_proj, d_gate_up, d_down = (
        lax.psum(d_mixer_in.astype(jnp.bfloat16), "dp").astype(jnp.float32),
        lax.psum(d_rate_proj.astype(jnp.bfloat16), "dp").astype(jnp.float32),
        lax.psum(d_conv.astype(jnp.bfloat16), "dp").astype(jnp.float32),
        lax.psum(d_decay.astype(jnp.bfloat16), "dp").astype(jnp.float32),
        lax.psum(d_bias.astype(jnp.bfloat16), "dp").astype(jnp.float32),
        lax.psum(d_out_proj.astype(jnp.bfloat16), "dp").astype(jnp.float32),
        lax.psum(d_gate_up.astype(jnp.bfloat16), "dp").astype(jnp.float32),
        lax.psum(d_down.astype(jnp.bfloat16), "dp").astype(jnp.float32),
    )
    d_attn_gain, d_ffn_gain, d_out_gain = lax.psum(
        (d_attn_gain, d_ffn_gain, d_out_gain), ("dp", "tensor")
    )
    layer_out = jnp.stack(results, axis=0)[None]
    d_tokens = jnp.stack(input_grads, axis=0)[None]
    return (
        layer_out,
        d_tokens,
        d_attn_gain,
        d_mixer_in,
        d_rate_proj,
        d_conv,
        d_decay,
        d_bias,
        d_out_gain,
        d_out_proj,
        d_ffn_gain,
        d_gate_up,
        d_down,
    )


def solution(mesh):
    in_specs = (
        P("dp", None, "tensor", None),
        P("dp", None),
        P("dp", None, "tensor", None),
        P(),
        P(None, None, "tensor"),
        P(None, None, "tensor"),
        P(None, None, "tensor"),
        P("tensor"),
        P("tensor"),
        P(),
        P("tensor", None),
        P(),
        P(None, None, "tensor"),
        P("tensor", None),
    )
    out_specs = (
        P("dp", None, "tensor", None),
        P("dp", None, "tensor", None),
        P(),
        P(None, None, "tensor"),
        P(None, None, "tensor"),
        P(None, None, "tensor"),
        P("tensor"),
        P("tensor"),
        P(),
        P("tensor", None),
        P(),
        P(None, None, "tensor"),
        P("tensor", None),
    )
    return jax.shard_map(shards, mesh=mesh, in_specs=in_specs, out_specs=out_specs, check_vma=False)
```

profile of v0, /device:TPU:1, one launch (start us, length us, event | category | flops | bytes accessed | tf_op | source)
XLA Modules:
  0.0 2155.5 jit_solution(16887801620935659313)
XLA Ops:
  13.4 53.9 %all-gather.9.cloned.1.call-done = bf16[512,2048]{1,0:T(8,128)(2,1)} async-done(((bf16[64,2048]{1,0:T(8,128)(2,1)}), bf16[512,2048]{1,0:T(8,128)(2,1)}) %all-gather.9.cloned.1.call-update) | async-done | bytes 2097168 | tf_op jit(solution)/shard_map/all_gather | solution.py:170
  75.1 45.9 %all-gather.13.cloned.1.call-done = bf16[512,2048]{1,0:T(8,128)(2,1)} async-done(((bf16[64,2048]{1,0:T(8,128)(2,1)}), bf16[512,2048]{1,0:T(8,128)(2,1)}) %all-gather.13.cloned.1.call-update) | async-done | bytes 2097168 | tf_op jit(solution)/shard_map/all_gather | solution.py:170
  275.6 57.2 %while.88 = (s32[]{:T(128)}, f32[2,128,128]{2,1,0:T(8,128)S(1)}, f32[8,2,64,128]{3,2,1,0:T(8,128)}, f32[8,2,128,128]{3,2,1,0:T(8,128)}, f32[8,2]{1,0:T(8,128)}, ...) while((s32[]{:T(128)}, f32[2,128,128]{2,1,0:T(8,128)S(1)}, ...), condition=%wide.region_5.7_spmd.clone, body=%wide.region_4.6_spmd.clone.sunk | while | flops 88326144 | bytes 1511613 | solution.py:98
  362.2 57.1 %while.89 = (s32[]{:T(128)}, f32[2,128,128]{2,1,0:T(8,128)S(1)}, f32[8,2,64,128]{3,2,1,0:T(8,128)}, f32[8,2,128,128]{3,2,1,0:T(8,128)}, f32[8,2]{1,0:T(8,128)}, ...) while((s32[]{:T(128)}, f32[2,128,128]{2,1,0:T(8,128)S(1)}, ...), condition=%wide.region_15.17_spmd.clone, body=%wide.region_14.16_spmd.clone.sunk | while | flops 88326144 | bytes 1511613 | solution.py:98
  435.7 86.3 %reduce-scatter.9.cloned.1.call-done = f32[64,2048]{1,0:T(8,128)} async-done(((f32[512,2048]{1,0:T(8,128)}), f32[64,2048]{1,0:T(8,128)}) %reduce-scatter.9.cloned.1.call-update) | async-done | bytes 524304 | tf_op jit(solution)/shard_map/reduce_scatter | solution.py:179
  522.0 94.1 %reduce-scatter.13.cloned.1.call-done = f32[64,2048]{1,0:T(8,128)} async-done(((f32[512,2048]{1,0:T(8,128)}), f32[64,2048]{1,0:T(8,128)}) %reduce-scatter.13.cloned.1.call-update) | async-done | bytes 524304 | tf_op jit(solution)/shard_map/reduce_scatter | solution.py:179
  624.2 48.3 %all-gather.11.cloned.1.call-done = bf16[512,2048]{1,0:T(8,128)(2,1)} async-done(((bf16[64,2048]{1,0:T(8,128)(2,1)}), bf16[512,2048]{1,0:T(8,128)(2,1)}) %all-gather.11.cloned.1.call-update) | async-done | bytes 2097168 | tf_op jit(solution)/shard_map/all_gather | solution.py:185
  672.4 8.0 fusion.96
  680.5 45.5 %all-gather.17.cloned.1.call-done = bf16[512,2048]{1,0:T(8,128)(2,1)} async-done(((bf16[64,2048]{1,0:T(8,128)(2,1)}), bf16[512,2048]{1,0:T(8,128)(2,1)}) %all-gather.17.cloned.1.call-update) | async-done | bytes 2097168 | tf_op jit(solution)/shard_map/all_gather | solution.py:197
  732.5 7.3 bitcast_convert_fusion.1
  739.9 51.9 %reduce-scatter.17.cloned.1.call-done = bf16[64,2048]{1,0:T(8,128)(2,1)} async-done(((bf16[512,2048]{1,0:T(8,128)(2,1)}), bf16[64,2048]{1,0:T(8,128)(2,1)}) %reduce-scatter.17.cloned.1.call-update) | async-done | bytes 262160 | tf_op jit(solution)/shard_map/reduce_scatter | solution.py:210
  795.8 50.4 %all-gather.15.cloned.1.call-done = bf16[512,2048]{1,0:T(8,128)(2,1)} async-done(((bf16[64,2048]{1,0:T(8,128)(2,1)}), bf16[512,2048]{1,0:T(8,128)(2,1)}) %all-gather.15.cloned.1.call-update) | async-done | bytes 2097168 | tf_op jit(solution)/shard_map/all_gather | solution.py:185
  846.1 8.0 fusion.87
  854.2 45.1 %all-gather.21.cloned.1.call-done = bf16[512,2048]{1,0:T(8,128)(2,1)} async-done(((bf16[64,2048]{1,0:T(8,128)(2,1)}), bf16[512,2048]{1,0:T(8,128)(2,1)}) %all-gather.21.cloned.1.call-update) | async-done | bytes 2097168 | tf_op jit(solution)/shard_map/all_gather | solution.py:197
  921.9 43.2 %reduce-scatter.21.cloned.1.call-done = bf16[64,2048]{1,0:T(8,128)(2,1)} async-done(((bf16[512,2048]{1,0:T(8,128)(2,1)}), bf16[64,2048]{1,0:T(8,128)(2,1)}) %reduce-scatter.21.cloned.1.call-update) | async-done | bytes 262160 | tf_op jit(solution)/shard_map/reduce_scatter | solution.py:210
  966.9 52.6 %reduce-scatter.11.cloned.1.call-done = bf16[64,2048]{1,0:T(8,128)(2,1)} async-done(((bf16[512,2048]{1,0:T(8,128)(2,1)}), bf16[64,2048]{1,0:T(8,128)(2,1)}) %reduce-scatter.11.cloned.1.call-update) | async-done | bytes 262160 | tf_op jit(solution)/shard_map/reduce_scatter | solution.py:189
  1019.4 54.7 %reduce-scatter.15.cloned.1.call-done = bf16[64,2048]{1,0:T(8,128)(2,1)} async-done(((bf16[512,2048]{1,0:T(8,128)(2,1)}), bf16[64,2048]{1,0:T(8,128)(2,1)}) %reduce-scatter.15.cloned.1.call-update) | async-done | bytes 262160 | tf_op jit(solution)/shard_map/reduce_scatter | solution.py:189
  1078.1 50.7 %all-gather.19.cloned.1.call-done = bf16[512,2048]{1,0:T(8,128)(2,1)} async-done(((bf16[64,2048]{1,0:T(8,128)(2,1)}), bf16[512,2048]{1,0:T(8,128)(2,1)}) %all-gather.19.cloned.1.call-update) | async-done | bytes 2097168 | tf_op jit(solution)/shard_map/all_gather | solution.py:219
  1132.2 50.1 %all-gather.23.cloned.1.call-done = bf16[512,2048]{1,0:T(8,128)(2,1)} async-done(((bf16[64,2048]{1,0:T(8,128)(2,1)}), bf16[512,2048]{1,0:T(8,128)(2,1)}) %all-gather.23.cloned.1.call-update) | async-done | bytes 2097168 | tf_op jit(solution)/shard_map/all_gather | solution.py:219
  1200.1 89.6 %while.90 = (s32[]{:T(128)}, f32[2,128,128]{2,1,0:T(8,128)S(1)}, f32[8,2,64,128]{3,2,1,0:T(8,128)}, f32[8,2,64,128]{3,2,1,0:T(8,128)S(1)}, f32[8,2,64,128]{3,2,1...) while((s32[]{:T(128)}, f32[2,128,128]{2,1,0:T(8,128)S(1)}, ...), condition=%wide.region_26.28_spmd.clone, body=%wide.region_23.27_spmd.clone.sunk | while | flops 226819968 | bytes 4493123 | solution.py:98
  1411.6 134.2 %while.91 = (s32[]{:T(128)}, f32[2,128,128]{2,1,0:T(8,128)S(1)}, f32[8,2,64,128]{3,2,1,0:T(8,128)}, f32[8,2,64,128]{3,2,1,0:T(8,128)}, f32[8,2,64,128]{3,2,1,0:T...) while((s32[]{:T(128)}, f32[2,128,128]{2,1,0:T(8,128)S(1)}, ...), condition=%wide.region_45.47_spmd.clone, body=%wide.region_42.46_spmd.clone.sunk | while | flops 226819968 | bytes 4495199 | solution.py:98
  1731.8 65.0 %all-reduce.413 = (bf16[3,4,256]{2,0,1:T(4,128)(2,1)S(1)}, bf16[2048,2,2]{0,2,1:T(2,128)(2,1)S(1)}, bf16[2]{0:T(256)(128)(2,1)S(1)}, bf16[2]{0:T(256)(128)(2,1)S(1)}) all-reduce(bf16[3,4,256]{2,0,1:T(4,128)(2,1)S(1)} %add_convert_fusion.9, bf16[2048,2,2]{0,2,1:T(2,128)(2,1)S(1)} %fusion.85, ...), channel_id=1, replica_groups=mesh['dp'=16,'tensor'=8] {'dp'}, use_global_device_ids=true, to_apply=%region_71.73 | all-reduce | flops 11268 | bytes 45072 | tf_op jit(solution)/shard_map/psum | solution.py:251
  1800.6 326.3 %all-reduce.412 = (f32[2048]{0:T(1024)}, f32[128]{0:T(128)}, f32[2048]{0:T(1024)}) all-reduce(f32[2048]{0:T(1024)S(1)} %add.1264, f32[128]{0:T(128)S(1)} %add.1270, f32[2048]{0:T(1024)S(1)} %add.1272), channel_id=1, replica_groups=mesh['dp'=16,'tensor'=8] {'dp','tensor'}, use_global_device_ids=true, to_apply=%region_60.62 | all-reduce | flops 4224 | bytes 33792 | tf_op jit(solution)/shard_map/psum | solution.py:258
  2129.4 8.5 copy.1646
  (2729 shorter events, 932.1 us)
Async XLA Ops:
  7.2 718.8 %copy-start = (bf16[704,2048]{1,0:T(8,128)(2,1)S(1)}, bf16[704,2048]{1,0:T(8,128)(2,1)}, u32[]{:S(2)}) copy-start(bf16[704,2048]{1,0:T(8,128)(2,1)} %param.36) | copy-start | bytes 8650756
  7.2 60.1 %all-gather.9.cloned.1.call-start = ((), (), s32[]{:S(2)}) async-start(), calls=%async_computation.8 | async-start | bytes 2359296 | tf_op jit(solution)/shard_map/all_gather | solution.py:170
  11.8 109.2 %all-gather.13.cloned.1.call-start = ((), (), s32[]{:S(2)}) async-start(), calls=%async_computation.12 | async-start | bytes 2359296 | tf_op jit(solution)/shard_map/all_gather | solution.py:170
  12.6 509.4 %reduce-scatter.9.cloned.1.call-start = ((), (), s32[]{:S(2)}) async-start(), calls=%async_computation.9 | async-start | bytes 4718592 | tf_op jit(solution)/shard_map/reduce_scatter | solution.py:179
  431.3 184.8 %reduce-scatter.13.cloned.1.call-start = ((), (), s32[]{:S(2)}) async-start(), calls=%async_computation.13 | async-start | bytes 4718592 | tf_op jit(solution)/shard_map/reduce_scatter | solution.py:179
  435.4 184.8 %copy-start.637 = (s32[1,2]{1,0:T(1,128)S(1)}, s32[1,2]{1,0:T(1,128)}, u32[]{:S(2)}) copy-start(s32[1,2]{1,0:T(1,128)} %param.24) | copy-start | bytes 28
  435.4 237.0 %all-gather.11.cloned.1.call-start = ((), (), s32[]{:S(2)}) async-start(), calls=%async_computation.10 | async-start | bytes 2359296 | tf_op jit(solution)/shard_map/all_gather | solution.py:185
  620.1 105.8 %all-gather.17.cloned.1.call-start = ((), (), s32[]{:S(2)}) async-start(), calls=%async_computation.16 | async-start | bytes 2359296 | tf_op jit(solution)/shard_map/all_gather | solution.py:197
  624.1 167.7 %reduce-scatter.17.cloned.1.call-start = ((), (), s32[]{:S(2)}) async-start(), calls=%async_computation.17 | async-start | bytes 2359296 | tf_op jit(solution)/shard_map/reduce_scatter | solution.py:210
  739.8 106.3 %all-gather.15.cloned.1.call-start = ((), (), s32[]{:S(2)}) async-start(), calls=%async_computation.14 | async-start | bytes 2359296 | tf_op jit(solution)/shard_map/all_gather | solution.py:185
  794.6 104.7 %all-gather.21.cloned.1.call-start = ((), (), s32[]{:S(2)}) async-start(), calls=%async_computation.20 | async-start | bytes 2359296 | tf_op jit(solution)/shard_map/all_gather | solution.py:197
  795.3 169.9 %reduce-scatter.21.cloned.1.call-start = ((), (), s32[]{:S(2)}) async-start(), calls=%async_computation.21 | async-start | bytes 2359296 | tf_op jit(solution)/shard_map/reduce_scatter | solution.py:210
  913.2 106.2 %reduce-scatter.11.cloned.1.call-start = ((), (), s32[]{:S(2)}) async-start(), calls=%async_computation.11 | async-start | bytes 2359296 | tf_op jit(solution)/shard_map/reduce_scatter | solution.py:189
  917.5 156.5 %reduce-scatter.15.cloned.1.call-start = ((), (), s32[]{:S(2)}) async-start(), calls=%async_computation.15 | async-start | bytes 2359296 | tf_op jit(solution)/shard_map/reduce_scatter | solution.py:189
  921.9 206.9 %all-gather.19.cloned.1.call-start = ((), (), s32[]{:S(2)}) async-start(), calls=%async_computation.18 | async-start | bytes 2359296 | tf_op jit(solution)/shard_map/all_gather | solution.py:219
  1077.2 105.1 %all-gather.23.cloned.1.call-start = ((), (), s32[]{:S(2)}) async-start(), calls=%async_computation.22 | async-start | bytes 2359296 | tf_op jit(solution)/shard_map/all_gather | solution.py:219
  1077.8 721.3 %reduce-scatter.19.cloned.1.call-start = ((), (), s32[]{:S(2)}) async-start(), calls=%async_computation.19 | async-start | bytes 2359296 | tf_op jit(solution)/shard_map/reduce_scatter | solution.py:239
  1289.7 347.0 %copy-start.30 = (f32[8,2,64,64]{3,2,1,0:T(8,128)}, f32[8,2,64,64]{3,2,1,0:T(8,128)S(1)}, u32[]{:S(2)}) copy-start(f32[8,2,64,64]{3,2,1,0:T(8,128)S(1)} %get-tuple-element.872) | copy-start | bytes 786436
  1683.5 115.6 %reduce-scatter.23.cloned.1.call-start = ((), (), s32[]{:S(2)}) async-start(), calls=%async_computation.23 | async-start | bytes 2359296 | tf_op jit(solution)/shard_map/reduce_scatter | solution.py:239
  1698.9 430.5 %all-reduce.417.cloned.1.call-start = ((), (), s32[]{:S(2)}) async-start(), calls=%async_computation.24 | async-start | bytes 27787264 | tf_op jit(solution)/shard_map/psum | solution.py:249
  1731.4 395.5 %copy-start.110 = (f32[64,2048]{1,0:T(8,128)S(1)}, f32[64,2048]{1,0:T(8,128)}, u32[]{:S(2)}) copy-start(f32[64,2048]{1,0:T(8,128)} %get-tuple-element.1622) | copy-start | bytes 1572868
  1731.4 395.5 %copy-start.111 = (f32[64,2048]{1,0:T(8,128)S(1)}, f32[64,2048]{1,0:T(8,128)}, u32[]{:S(2)}) copy-start(f32[64,2048]{1,0:T(8,128)} %get-tuple-element.1676) | copy-start | bytes 1572868
  1731.4 395.5 %copy-start.640 = (f32[64]{0:T(128)S(1)}, f32[64]{0:T(128)}, u32[]{:S(2)}) copy-start(f32[64]{0:T(128)} %get-tuple-element.1911) | copy-start | bytes 772
  1731.4 395.5 %copy-start.641 = (f32[64]{0:T(128)S(1)}, f32[64]{0:T(128)}, u32[]{:S(2)}) copy-start(f32[64]{0:T(128)} %get-tuple-element.1913) | copy-start | bytes 772
  (677 other events, 8444.8 us)
Sparse Core Ops, SparseCore 0:
  11.9 55.3 all-gather.8
  69.5 51.4 all-gather.12
  431.4 90.5 reduce-scatter.8
  524.8 91.2 reduce-scatter.12
  620.3 52.1 all-gather.10
  674.5 51.4 all-gather.16
  739.9 51.8 reduce-scatter.16
  794.7 51.3 all-gather.14
  847.8 51.4 all-gather.20
  913.3 51.8 reduce-scatter.20
  967.6 51.7 reduce-scatter.10
  1022.2 51.7 reduce-scatter.14
  1077.3 51.3 all-gather.18
  1130.9 51.4 all-gather.22
  1683.6 51.8 reduce-scatter.18
  1737.8 52.6 reduce-scatter.22
  1794.2 310.4 all-reduce.416
where the time goes:
time: 2180 us; the launch traced here: 2160 us
  waiting for transfers between devices  775 us (36%)
  matrix products  562 us (26%)
  blocking collectives  391 us (18%)
  local copies, waits for them, and re-layouts  257 us (12%)
  other arithmetic  142 us (7%)
  between operations  25.9 us (1%)
    psum x1, blocking collectives, shards(): lax.psum((d_attn_gain, d_ffn_gain, d_out_gain), ('dp', 'tensor'))  326 us
    reduce_scatter x2, waiting for transfers between devices, shards(): lax.psum_scatter(rows_product(mixer_rows, out_proj), 'tensor', scatter_di...  180 us
    dot_general x186, matrix products, unit_lower_inverse(): jnp.einsum('...ij,...jk->...ik', lower[..., half:, :half], top, precision...  118 us
    reduce_scatter x2, waiting for transfers between devices, shards(): lax.psum_scatter(rows_product(inner, down_proj).astype(jnp.bfloat16), 'te...  107 us
    dot_general x186, matrix products, unit_lower_inverse(): corner = -jnp.einsum('...ij,...jk->...ik', bottom, middle, precision=HIGH)  107 us
    all_gather x2, waiting for transfers between devices, shards(): lax.all_gather(d_hidden.astype(jnp.bfloat16), 'tensor', axis=0, tiled=True)  101 us
    all_gather x2, waiting for transfers between devices, shards(): rows_one = lax.all_gather(normed_one, 'tensor', axis=0, tiled=True)  99.7 us
    all_gather x2, waiting for transfers between devices, shards(): rows_two = lax.all_gather(normed_two, 'tensor', axis=0, tiled=True)  98.6 us
  transfers between devices with their start and end apart: 17, of which 14 were waited for; matrix products, arithmetic and copies ran while one was open for 4% of the time, Pallas kernels for 0%

commit v1 on v0

v1 whole, which is shorter than its diff:
```python
import jax, jax.numpy as jnp
from jax import lax
from jax.experimental import pallas as pl
from jax.experimental.pallas import tpu as pltpu
from jax.sharding import Mesh, PartitionSpec as P

EPS = 1e-06
BLOCK = 64
HS = 128
HEADS = 2
WIDTH = HEADS * HS
F32 = jnp.float32
HIGHEST = lax.Precision.HIGHEST
HIGH = lax.Precision.HIGH
LOW = lax.Precision.DEFAULT
P_INV = HIGH
P_ST = HIGH
P_GR = HIGH


def dot2(a, b, ca, cb, precision):
    return lax.dot_general(a, b, (((ca,), (cb,)), ((), ())), precision=precision, preferred_element_type=F32)


def bdot(a, b, ca, cb, precision):
    if precision == LOW:
        a, b = a.astype(jnp.bfloat16), b.astype(jnp.bfloat16)
    return jnp.stack([dot2(a[i], b[i], ca, cb, precision) for i in range(a.shape[0])])


def split_heads(rows):
    blocks = rows.shape[0] // BLOCK
    return jnp.concatenate(
        [rows[:, h * HS : (h + 1) * HS].reshape(blocks, BLOCK, HS) for h in range(HEADS)], axis=0
    )


def join_heads(stacked):
    blocks = stacked.shape[0] // HEADS
    return jnp.concatenate(
        [stacked[h * blocks : (h + 1) * blocks].reshape(blocks * BLOCK, HS) for h in range(HEADS)], axis=1
    )


def shift_down(rows, steps):
    if steps == 0:
        return rows
    place = lax.broadcasted_iota(jnp.int32, rows.shape, 0)
    return jnp.where(place >= steps, pltpu.roll(rows, steps, 0), 0.0)


def shift_up(rows, steps):
    if steps == 0:
        return rows
    size = rows.shape[0]
    place = lax.broadcasted_iota(jnp.int32, rows.shape, 0)
    return jnp.where(place < size - steps, pltpu.roll(rows, size - steps, 0), 0.0)


def sigmoid(v):
    return 1.0 / (1.0 + jnp.exp(-v))


def softplus(v):
    return jnp.maximum(v, 0.0) + jnp.log1p(jnp.exp(-jnp.abs(v)))


def convolve(rows, taps):
    out = rows * taps[3:4, :]
    for j in range(3):
        out = out + shift_down(rows, 3 - j) * taps[j : j + 1, :]
    return out


def columns(table, blocks, first):
    return jnp.concatenate(
        [table[:, first + h : first + h + 1].reshape(blocks, BLOCK, 1) for h in range(HEADS)], axis=0
    )


def rows_of(turned, first):
    return jnp.concatenate([turned[:, first + h : first + h + 1, :] for h in range(HEADS)], axis=0)


def gates(rates, decay_rate, decay_bias):
    blocks = rates.shape[0] // BLOCK
    soft = softplus(rates + decay_bias)
    logdecay = (-decay_rate * soft).reshape(blocks, BLOCK, 128)
    row = lax.broadcasted_iota(jnp.int32, (BLOCK, BLOCK), 0)
    col = lax.broadcasted_iota(jnp.int32, (BLOCK, BLOCK), 1)
    ones = (row >= col).astype(F32)
    cumul = jnp.stack([dot2(ones, logdecay[n], 1, 0, HIGHEST) for n in range(blocks)])
    update = sigmoid(rates).reshape(blocks, BLOCK, 128)
    lane = lax.broadcasted_iota(jnp.int32, (blocks, BLOCK, 128), 2)
    table = jnp.where(lane < 2, cumul, update)
    turned = jnp.stack([jnp.transpose(table[n], (1, 0)) for n in range(blocks)])
    flat = table.reshape(blocks * BLOCK, 128)
    return soft, columns(flat, blocks, 0), rows_of(turned, 0), columns(flat, blocks, 2), rows_of(turned, 2)


def activate(rows, taps):
    pre = convolve(rows, taps)
    sig = sigmoid(pre)
    return pre, sig, pre * sig


def lower_inverse(strict):
    row = lax.broadcasted_iota(jnp.int32, strict.shape, 1)
    col = lax.broadcasted_iota(jnp.int32, strict.shape, 2)
    size = 1
    inverse = jnp.where(row == col, 1.0, 0.0)
    while size < BLOCK:
        lower = jnp.where((row // (2 * size) == col // (2 * size)) & (row // size != col // size), strict, 0.0)
        if size == 1:
            inverse = inverse - lower
        else:
            inverse = inverse - bdot(inverse, bdot(lower, inverse, 2 - 1, 0, P_INV), 1, 0, P_INV)
        size *= 2
    return inverse


def parts(queries, keys, cum_c, cum_r, upd_r):
    shape = (queries.shape[0], BLOCK, BLOCK)
    row = lax.broadcasted_iota(jnp.int32, shape, 1)
    col = lax.broadcasted_iota(jnp.int32, shape, 2)
    both = bdot(jnp.concatenate([keys, queries], axis=1), keys, 1, 1, P_GR)
    ratio = jnp.where(row >= col, jnp.exp(jnp.where(row >= col, cum_c - cum_r, 0.0)), 0.0)
    scaled = ratio * upd_r
    return row, col, scaled, ratio, both[:, :BLOCK], both[:, BLOCK:]


def unit(v):
    return lax.rsqrt(jnp.sum(v * v, -1, keepdims=True) + EPS)


def in_order(slots, source, target):
    for n in range(target.shape[0] // BLOCK):
        target[n * BLOCK : (n + 1) * BLOCK, :] = source[pl.ds(pl.multiple_of(slots[n] * BLOCK, BLOCK), BLOCK), :]


def to_slots(slots, rows, target, lanes):
    for n in range(rows.shape[0] // BLOCK):
        target[pl.ds(pl.multiple_of(slots[n] * BLOCK, BLOCK), BLOCK), lanes] = rows[n * BLOCK : (n + 1) * BLOCK]


def fwd_kernel(
    slots, mixed_ref, conv_ref, dec_ref, gain_ref,
    rows_ref, out_ref, err_ref, inv_ref, sk_ref, state_ref, step_ref, proj_ref,
):
    width = WIDTH
    in_order(slots, mixed_ref, proj_ref)
    _, _, act_q = activate(proj_ref[:, 0:width], conv_ref[0])
    _, _, act_k = activate(proj_ref[:, width : 2 * width], conv_ref[1])
    _, _, act_v = activate(proj_ref[:, 2 * width : 3 * width], conv_ref[2])
    act_q, act_k, values = split_heads(act_q), split_heads(act_k), split_heads(act_v)
    queries = act_q * (unit(act_q) * HS**-0.5)
    keys = act_k * unit(act_k)
    _, cum_c, cum_r, upd_c, upd_r = gates(proj_ref[:, 4 * width :], dec_ref[0:1, :], dec_ref[1:2, :])
    row, col, scaled, _, kk, qk = parts(queries, keys, cum_c, cum_r, upd_r)
    inverse = lower_inverse(jnp.where(row > col, scaled * kk, 0.0))
    inv_ref[...] = inverse
    attend = scaled * qk
    grow = jnp.exp(cum_c)
    last = cum_c[:, BLOCK - 1 :, :]
    tail = keys * (jnp.exp(last - cum_c) * upd_c)
    solved = bdot(inverse, jnp.concatenate([values, grow * keys], axis=2), 1, 0, P_ST)
    sk_ref[...] = solved[:, :, HS:]
    carried = bdot(tail, solved, 0, 0, P_ST)
    n = carried.shape[0]
    row2 = lax.broadcasted_iota(jnp.int32, (n, HS, HS), 1)
    col2 = lax.broadcasted_iota(jnp.int32, (n, HS, HS), 2)
    step = jnp.where(row2 == col2, jnp.exp(last), 0.0) - carried[:, :, HS:]
    step_ref[...] = step
    blocks = n // HEADS
    states = []
    for h in range(HEADS):
        state = jnp.zeros((HS, HS), F32)
        states.append(state)
        for i in range(blocks - 1):
            at = h * blocks + i
            state = carried[at, :, :HS] + (dot2(step[at], state, 1, 0, P_ST) if i else 0.0)
            states.append(state)
    states = jnp.stack(states)
    state_ref[...] = states
    seen = bdot(jnp.concatenate([solved[:, :, HS:], grow * queries], axis=1), states, 1, 0, P_ST)
    errors = solved[:, :, :HS] - seen[:, :BLOCK]
    err_ref[...] = errors
    outputs = seen[:, BLOCK:] + bdot(attend, errors, 1, 0, P_ST)
    out_ref[...] = outputs
    scale = lax.rsqrt(jnp.mean(outputs * outputs, -1, keepdims=True) + EPS)
    gate = proj_ref[:, 3 * width : 4 * width]
    rows = (join_heads(outputs * scale * gain_ref[...]) * (gate * sigmoid(gate))).astype(jnp.bfloat16)
    to_slots(slots, rows, rows_ref, slice(0, width))


def unit_back(act, d_norm, factor):
    r = unit(act)
    return factor * (r * d_norm - act * (r * r * r) * jnp.sum(d_norm * act, -1, keepdims=True))


def bwd_kernel(
    slots, mixed_ref, conv_ref, dec_ref, gain_ref, drows_mixed_ref,
    out_ref, err_ref, inv_ref, sk_ref, state_ref, step_ref,
    dproj_ref, dconv_ref, dsmall_ref, proj_ref, drows_ref,
):
    width = WIDTH
    in_order(slots, mixed_ref, proj_ref)
    in_order(slots, drows_mixed_ref, drows_ref)
    n = err_ref.shape[0]
    blocks = n // HEADS
    rates = proj_ref[:, 4 * width :]
    pre_q, sig_q, full_q = activate(proj_ref[:, 0:width], conv_ref[0])
    pre_k, sig_k, full_k = activate(proj_ref[:, width : 2 * width], conv_ref[1])
    act_q, act_k = split_heads(full_q), split_heads(full_k)
    queries = act_q * (unit(act_q) * HS**-0.5)
    keys = act_k * unit(act_k)
    soft, cum_c, cum_r, upd_c, upd_r = gates(rates, dec_ref[0:1, :], dec_ref[1:2, :])
    row, col, scaled, ratio, kk, qk = parts(queries, keys, cum_c, cum_r, upd_r)
    attend = scaled * qk
    grow = jnp.exp(cum_c)
    last = cum_c[:, BLOCK - 1 :, :]
    fade = jnp.exp(last - cum_c)
    weight = fade * upd_c
    tail = keys * weight
    outputs, errors, states = out_ref[...], err_ref[...], state_ref[...]

    gate = proj_ref[:, 3 * width : 4 * width]
    sig_g = sigmoid(gate)
    d_rows = drows_ref[...]
    scale = lax.rsqrt(jnp.mean(outputs * outputs, -1, keepdims=True) + EPS)
    gain = gain_ref[...]
    normal = outputs * scale
    d_gained = split_heads(d_rows * (gate * sig_g))
    d_gate = d_rows * join_heads(normal * gain) * (sig_g * (1.0 + gate * (1.0 - sig_g)))
    to_slots(slots, d_gate.astype(jnp.bfloat16), dproj_ref, slice(3 * width, 4 * width))
    d_gain = jnp.sum((d_gained * normal).reshape(n * BLOCK, HS), 0, keepdims=True)
    d_normal = d_gained * gain
    d_out = scale * d_normal - outputs * (scale * scale * scale) * jnp.mean(d_normal * outputs, -1, keepdims=True)

    d_err_own = bdot(attend, d_out, 0, 0, P_ST)
    to_state = bdot(
        jnp.concatenate([grow * queries, -sk_ref[...]], axis=1),
        jnp.concatenate([d_out, d_err_own], axis=1), 0, 0, P_ST,
    )
    d_ends = [None] * n
    for h in range(HEADS):
        d_end = jnp.zeros((HS, HS), F32)
        for i in range(blocks - 1, -1, -1):
            at = h * blocks + i
            d_ends[at] = d_end
            if i:
                d_end = to_state[at] + (dot2(step_ref[at], d_end, 0, 0, P_ST) if i < blocks - 1 else 0.0)
    d_ends = jnp.stack(d_ends)
    d_err = d_err_own + bdot(tail, d_ends, 1, 0, P_ST)
    d_val = bdot(inv_ref[...], d_err, 0, 0, P_ST)
    pair = jnp.concatenate([d_out, d_val], axis=1)
    by_err = bdot(pair, errors, 1, 1, P_GR)
    by_state = bdot(pair, states, 1, 1, P_GR)
    d_tail = bdot(errors, d_ends, 1, 1, P_GR)
    raw_attend = jnp.where(row >= col, by_err[:, :BLOCK], 0.0)
    raw_system = jnp.where(row > col, -by_err[:, BLOCK:], 0.0)
    d_qk = raw_attend * scaled
    d_kk = raw_system * scaled
    d_seen_q, d_seen_k = by_state[:, :BLOCK], -by_state[:, BLOCK:]
    stacked = jnp.concatenate([d_qk, d_kk], axis=1)
    from_left = bdot(stacked, keys, 1, 0, P_GR)
    from_right = bdot(stacked, jnp.concatenate([queries, keys], axis=1), 0, 0, P_GR)
    d_queries = grow * d_seen_q + from_left[:, :BLOCK]
    d_keys = grow * d_seen_k + weight * d_tail + from_left[:, BLOCK:] + from_right

    mixed = ratio * (raw_attend * qk + raw_system * kk)
    moved = mixed * upd_r
    eye = row == col
    over_upd = jnp.sum(mixed, 1, keepdims=True)
    tail_dot = jnp.sum(keys * d_tail, -1, keepdims=True)
    tail_part = weight * tail_dot
    d_upd = jnp.sum(jnp.where(eye, over_upd, 0.0), -1, keepdims=True) + fade * tail_dot
    d_cum = jnp.sum(moved - jnp.where(eye, over_upd * upd_r, 0.0), -1, keepdims=True)
    d_cum = d_cum + grow * jnp.sum(d_seen_q * queries + d_seen_k * keys, -1, keepdims=True) - tail_part
    d_last = jnp.sum(tail_part, 1, keepdims=True) + jnp.exp(last) * jnp.sum(
        jnp.sum(states * d_ends, 1, keepdims=True), 2, keepdims=True
    )
    ones = (lax.broadcasted_iota(jnp.int32, (BLOCK, BLOCK), 0) <= lax.broadcasted_iota(jnp.int32, (BLOCK, BLOCK), 1)).astype(F32)
    lane = lax.broadcasted_iota(jnp.int32, (blocks, BLOCK, 128), 2)
    spread = jnp.where(lane == 0, d_cum[:blocks], jnp.where(lane == 1, d_cum[blocks:], 0.0))
    d_log = jnp.stack([dot2(ones, spread[i], 1, 0, HIGHEST) for i in range(blocks)])
    d_log = d_log + jnp.where(lane == 0, d_last[:blocks], jnp.where(lane == 1, d_last[blocks:], 0.0))
    d_update = jnp.where(lane == 2, d_upd[:blocks], jnp.where(lane == 3, d_upd[blocks:], 0.0))
    d_log = d_log.reshape(blocks * BLOCK, 128)
    d_update = d_update.reshape(blocks * BLOCK, 128)
    update = sigmoid(rates)
    decay_rate, decay_bias = dec_ref[0:1, :], dec_ref[1:2, :]
    d_first = d_log * -decay_rate * sigmoid(rates + decay_bias)
    d_rates = (d_first + d_update * update * (1.0 - update)).astype(jnp.bfloat16)
    to_slots(slots, d_rates, dproj_ref, slice(4 * width, 4 * width + 128))
    small = jnp.concatenate(
        [
            jnp.sum(d_log * -soft, 0, keepdims=True),
            jnp.sum(d_first, 0, keepdims=True),
            d_gain,
            jnp.zeros((5, 128), F32),
        ],
        axis=0,
    )
    dsmall_ref[...] = small

    for c, (pre, sig, d_act) in enumerate(
        (
            (pre_q, sig_q, join_heads(unit_back(act_q, d_queries, HS**-0.5))),
            (pre_k, sig_k, join_heads(unit_back(act_k, d_keys, 1.0))),
            (None, None, join_heads(d_val)),
        )
    ):
        rows = proj_ref[:, c * width : (c + 1) * width]
        taps = conv_ref[c]
        if pre is None:
            pre, sig, _ = activate(rows, taps)
        d_pre = d_act * (sig * (1.0 + pre * (1.0 - sig)))
        d_in = d_pre * taps[3:4, :]
        sums = []
        for j in range(3):
            d_in = d_in + shift_up(d_pre, 3 - j) * taps[j : j + 1, :]
            sums.append(jnp.sum(d_pre * shift_down(rows, 3 - j), 0, keepdims=True))
        sums.append(jnp.sum(d_pre * rows, 0, keepdims=True))
        to_slots(slots, d_in.astype(jnp.bfloat16), dproj_ref, slice(c * width, (c + 1) * width))
        dconv_ref[c] = jnp.concatenate(sums, axis=0)


def whole(shape):
    return pl.BlockSpec(tuple(shape), lambda i, slots: (0,) * len(shape))


def kernel_call(kernel, name, outs, ins, scratch):
    slots, rest = ins[0], ins[1:]
    return pl.pallas_call(
        kernel,
        grid_spec=pltpu.PrefetchScalarGridSpec(
            num_scalar_prefetch=1,
            grid=(1,),
            in_specs=[whole(a.shape) for a in rest],
            out_specs=[whole(o.shape) for o in outs],
            scratch_shapes=[pltpu.VMEM(shape, F32) for shape in scratch],
        ),
        out_shape=outs,
        compiler_params=pltpu.CompilerParams(vmem_limit_bytes=48 * 2**20),
        name=name,
    )(slots, *rest)


def mixer_fwd(slots, mixed, conv, dec, gain):
    positions = mixed.shape[0]
    n = HEADS * positions // BLOCK
    outs = [jax.ShapeDtypeStruct((positions, WIDTH), jnp.bfloat16)] + [
        jax.ShapeDtypeStruct(shape, F32)
        for shape in (
            (n, BLOCK, HS), (n, BLOCK, HS), (n, BLOCK, BLOCK), (n, BLOCK, HS), (n, HS, HS), (n, HS, HS),
        )
    ]
    return kernel_call(fwd_kernel, "mixer_fwd", outs, (slots, mixed, conv, dec, gain), [mixed.shape])


def mixer_bwd(slots, mixed, conv, dec, gain, d_rows, saved):
    outs = [
        jax.ShapeDtypeStruct(mixed.shape, jnp.bfloat16),
        jax.ShapeDtypeStruct(conv.shape, F32),
        jax.ShapeDtypeStruct((8, 128), F32),
    ]
    ins = (slots, mixed, conv, dec, gain, d_rows, *saved)
    return kernel_call(bwd_kernel, "mixer_bwd", outs, ins, [mixed.shape, d_rows.shape])


UP = [(i, (i + 1) % 4) for i in range(4)]
DOWN = [(i, (i - 1) % 4) for i in range(4)]
SWAP = [(0, 1), (1, 0)]
LOWP = jnp.bfloat16


def up(a):
    return lax.ppermute(a, "z", UP)


def down(a):
    return lax.ppermute(a, "z", DOWN)


def across(a):
    return lax.ppermute(a, "yl", SWAP)


def cuts(rows):
    first = (rows // 3 + 15) // 16 * 16
    return first, 2 * first


def gather(own):
    s, t = cuts(own.shape[0])
    b0, am, ap = across(own), up(own), down(own)
    bm, a2, bp = up(b0), down(ap), across(ap)
    return jnp.concatenate([own, b0, ap, bp, a2, up(bm[:s]), down(bp[s:t]), across(a2[t:]), am, bm], axis=0)


def add(*parts):
    total = parts[0].astype(F32)
    for part in parts[1:]:
        total = total + part.astype(F32)
    return total


def scatter(whole):
    rows = whole.shape[0] // 8
    s, t = cuts(rows)
    a0, b0, ap, bp, a2, b2, am, bm = (whole[i * rows : (i + 1) * rows] for i in range(8))
    r1, r2, r3 = down(b2[:s]), up(b2[s:t]), across(b2[t:])
    bm = jnp.concatenate([add(bm[:s], r1).astype(LOWP), bm[s:]], axis=0)
    bp = jnp.concatenate([bp[:s], add(bp[s:t], r2).astype(LOWP), bp[t:]], axis=0)
    a2 = jnp.concatenate([a2[:t], add(a2[t:], r3).astype(LOWP)], axis=0)
    q1, q2, q3 = down(bm), up(a2), across(bp)
    b0, ap = add(b0, q1).astype(LOWP), add(ap, q2, q3).astype(LOWP)
    return add(a0, across(b0), down(am), up(ap))


def dot(a, b, ca, cb):
    return lax.dot_general(a, b, (((ca,), (cb,)), ((), ())), preferred_element_type=F32)


def rms(v):
    return lax.rsqrt(jnp.mean(v * v, -1, keepdims=True) + EPS)


def norm_back(values, scale, gain, d_normed):
    weighted = d_normed * gain
    d_gain = jnp.sum(d_normed * values * scale, 0)
    d_values = scale * weighted - values * scale**3 * jnp.mean(weighted * values, -1, keepdims=True)
    return d_values, d_gain


def reduce_rows(rows):
    part = lax.psum_scatter(rows, "c", scatter_dimension=0, tiled=True)
    part = lax.psum_scatter(part, "x", scatter_dimension=0, tiled=True)
    part = add(part, lax.ppermute(part, "yh", SWAP)).astype(LOWP)
    part = lax.all_gather(part, "x", axis=0, tiled=True)
    return lax.all_gather(part, "c", axis=0, tiled=True)


def shards(
    tokens, lengths, cotangent, attn_gain, mixer_in, rate_proj, conv_weight, decay_rate, decay_bias,
    out_gain, out_proj, ffn_gain, gate_up, down_proj,
):
    rows = tokens.shape[2]
    micros = range(tokens.shape[1])
    z, yl = lax.axis_index("z"), lax.axis_index("yl")
    places = (2 * z + yl) * rows + jnp.arange(rows, dtype=jnp.int32)
    block = jnp.arange(8, dtype=jnp.int32)
    slots = 2 * ((block // 2 - z) % 4) + (block % 2 + yl) % 2

    width = mixer_in.shape[1] * mixer_in.shape[2]
    rate_pad = jnp.pad(rate_proj.reshape(rate_proj.shape[0], 4), ((0, 0), (0, 124)))
    w_in = jnp.concatenate([mixer_in.reshape(mixer_in.shape[0], width), rate_pad], axis=1)
    hidden_units = down_proj.shape[0]
    w_gate, w_up = gate_up[:, 0, :].T, gate_up[:, 1, :].T
    dec = jnp.pad(jnp.stack([decay_rate, decay_bias]), ((0, 0), (0, 126)))
    gain_row = out_gain[None]

    source = [tokens[0, m].astype(F32) for m in micros]
    valid = [(places < lengths[0, m]).astype(F32)[:, None] for m in micros]
    scale_one = [rms(source[m]) for m in micros]
    rows_one = [gather((source[m] * scale_one[m] * attn_gain).astype(LOWP)) for m in micros]
    grad_out = [cotangent[0, m].astype(F32) * valid[m] for m in micros]
    grad_rows = [gather(grad_out[m].astype(LOWP)) for m in micros]

    mixed, saved, mixer_rows, hidden, scale_two, rows_two = [], [], [], [], [], []
    for m in micros:
        mixed.append(dot(rows_one[m], w_in, 1, 0))
        out, *keep = mixer_fwd(slots, mixed[m], conv_weight, dec, gain_row)
        mixer_rows.append(out)
        saved.append(keep)
        attended = scatter(dot(out, out_proj, 1, 0).astype(LOWP))
        hidden.append(source[m] + attended)
        scale_two.append(rms(hidden[m]))
        rows_two.append(gather((hidden[m] * scale_two[m] * ffn_gain).astype(LOWP)))

    layer_out, d_hidden, grad_attn = [], [], []
    d_ffn_gain = 0.0
    d_down, d_gate, d_up = 0.0, 0.0, 0.0
    for m in micros:
        gate = dot(w_gate, rows_two[m], 1, 1)
        lift = dot(w_up, rows_two[m], 1, 1)
        sigma = jax.nn.sigmoid(gate)
        inner = (gate * sigma * lift).astype(LOWP)
        branch = scatter(dot(inner, down_proj, 0, 0).astype(LOWP))
        layer_out.append(((hidden[m] + branch) * valid[m]).astype(LOWP))
        d_inner = dot(down_proj, grad_rows[m], 1, 1)
        dg = (d_inner * lift * sigma * (1.0 + gate * (1.0 - sigma))).astype(LOWP)
        du = (d_inner * gate * sigma).astype(LOWP)
        d_normed = (dot(dg, w_gate, 0, 0) + dot(du, w_up, 0, 0)).astype(LOWP)
        d_normed = scatter(d_normed)
        d_down = d_down + dot(inner, grad_rows[m], 1, 0)
        d_gate = d_gate + dot(dg, rows_two[m], 1, 0)
        d_up = d_up + dot(du, rows_two[m], 1, 0)
        d_from, part = norm_back(hidden[m], scale_two[m], ffn_gain, d_normed)
        d_ffn_gain = d_ffn_gain + part
        d_hidden.append(grad_out[m] + d_from)
        grad_attn.append(gather(d_hidden[m].astype(LOWP)))
    ffn = reduce_rows(jnp.concatenate([d_gate.astype(LOWP), d_up.astype(LOWP), d_down.astype(LOWP)], axis=0))

    d_tokens = []
    d_attn_gain, d_conv, d_small, d_out, d_in = 0.0, 0.0, 0.0, 0.0, 0.0
    for m in micros:
        d_out = d_out + dot(mixer_rows[m], grad_attn[m], 0, 0)
        d_mixer_rows = dot(grad_attn[m], out_proj, 1, 1)
        d_mixed, conv_part, small_part = mixer_bwd(slots, mixed[m], conv_weight, dec, gain_row, d_mixer_rows, saved[m])
        d_normed = scatter(dot(d_mixed, w_in, 1, 1).astype(LOWP))
        d_in = d_in + dot(rows_one[m], d_mixed, 0, 0)
        d_conv, d_small = d_conv + conv_part, d_small + small_part
        d_from, part = norm_back(source[m], scale_one[m], attn_gain, d_normed)
        d_attn_gain = d_attn_gain + part
        d_tokens.append((d_hidden[m] + d_from).astype(LOWP))
    d_out = reduce_rows(d_out.astype(LOWP))
    d_mixer_in = reduce_rows(d_in[:, :width].astype(LOWP))
    dp = ("x", "yh", "c")
    d_rate, d_conv, d_pair = lax.psum(
        (d_in[:, width : width + 4], d_conv, d_small[:2, :2]), dp
    )
    d_attn_gain, d_ffn_gain, d_out_gain = lax.psum((d_attn_gain, d_ffn_gain, d_small[2]), dp + ("z", "yl"))
    ffn = ffn.astype(F32)
    d_gate_up = ffn[: 2 * hidden_units].reshape(2, hidden_units, -1).transpose(2, 0, 1)
    return (
        jnp.stack(layer_out)[None],
        jnp.stack(d_tokens)[None],
        d_attn_gain,
        d_mixer_in.astype(F32).reshape(mixer_in.shape),
        d_rate.reshape(rate_proj.shape),
        d_conv,
        d_pair[0],
        d_pair[1],
        d_out_gain,
        d_out.astype(F32),
        d_ffn_gain,
        d_gate_up,
        ffn[2 * hidden_units :],
    )


def solution(mesh):
    fine = Mesh(mesh.devices.reshape(4, 2, 2, 4, 2), ("x", "yh", "c", "z", "yl"))
    dp, tensor = ("x", "yh", "c"), ("z", "yl")
    in_specs = (
        P(dp, None, tensor, None),
        P(dp, None),
        P(dp, None, tensor, None),
        P(),
        P(None, None, tensor),
        P(None, None, tensor),
        P(None, None, tensor),
        P(tensor),
        P(tensor),
        P(),
        P(tensor, None),
        P(),
        P(None, None, tensor),
        P(tensor, None),
    )
    out_specs = (
        P(dp, None, tensor, None),
        P(dp, None, tensor, None),
        P(),
        P(None, None, tensor),
        P(None, None, tensor),
        P(None, None, tensor),
        P(tensor),
        P(tensor),
        P(),
        P(tensor, None),
        P(),
        P(None, None, tensor),
        P(tensor, None),
    )
    return jax.shard_map(shards, mesh=fine, in_specs=in_specs, out_specs=out_specs, check_vma=False)
```

time: 2180 us -> 907 us (0.42)
  matrix products: 562 us -> 66.7 us
  waiting for transfers between devices: 775 us -> 403 us
  blocking collectives: 391 us -> 152 us
  local copies, waits for them, and re-layouts: 257 us -> 53.4 us
  starting transfers between devices: 1.66 us -> 125 us
  other arithmetic: 142 us -> 36 us
  Pallas kernels: 0 us -> 47.1 us
    dot_general x650 -> x30, matrix products: 562 us -> 66.7 us  [dot(): lax.dot_general(a, b, (((ca,), (cb,)), ((), ())), preferred_element_type=...]
    all_gather x8 -> x5, waiting for transfers between devices: 390 us -> 66.3 us  [the longest x2 66.3 us: reduce_rows(): part = lax.all_gather(part, 'x', axis=0, tiled=True)]
    reduce_scatter x8 -> x6, waiting for transfers between devices: 383 us -> 126 us  [the longest x3 66.2 us: reduce_rows(): part = lax.psum_scatter(part, 'x', scatter_dimension=0, tiled=True)]
    psum x2, blocking collectives: 391 us -> 138 us  [the longest x1 69.3 us: shards(): lax.psum((d_in[:, width:width + 4], d_conv, d_small[:2, :2]), dp)]
    ppermute x0 -> x131, waiting for transfers between devices: none -> 211 us  [the longest x48 71.4 us: up(): return lax.ppermute(a, 'z', UP)]
    ppermute x0 -> x131, starting transfers between devices: none -> 124 us  [the longest x48 67.9 us: down(): return lax.ppermute(a, 'z', DOWN)]
    squeeze x98 -> x2, local copies, waits for them, and re-layouts: 90.7 us -> 0.52 us  [the longest x1 0.52 us: shards(): d_pair[1]]
    pallas_call x0 -> x4, Pallas kernels: none -> 47.1 us  [kernel_call(): pl.pallas_call(kernel, grid_spec=pltpu.PrefetchScalarGridSpec(num_scalar_...]
  transfers between devices with their start and end apart: 17 -> 142, of which waited for: 14 -> 69; matrix products, arithmetic and copies ran while one was open for 4% -> 12% of each run, Pallas kernels for 0% -> 4%
where the time goes in v1:
time: 907 us; the launch traced here: 899 us
  waiting for transfers between devices  403 us (44%)
  blocking collectives  152 us (17%)
  starting transfers between devices  125 us (14%)
  matrix products  66.7 us (7%)
  local copies, waits for them, and re-layouts  53.4 us (6%)
  Pallas kernels  47.1 us (5%)
  other arithmetic  36 us (4%)
  between operations  16.4 us (2%)
    ppermute x48, waiting for transfers between devices, up(): return lax.ppermute(a, 'z', UP)  71.4 us
    psum x1, blocking collectives, shards(): lax.psum((d_in[:, width:width + 4], d_conv, d_small[:2, :2]), dp)  69.3 us
    psum x1, blocking collectives, shards(): lax.psum((d_attn_gain, d_ffn_gain, d_small[2]), dp + ('z', 'yl'))  68.9 us
    ppermute x48, starting transfers between devices, down(): return lax.ppermute(a, 'z', DOWN)  67.9 us
    dot_general x30, matrix products, dot(): lax.dot_general(a, b, (((ca,), (cb,)), ((), ())), preferred_element_type=...  66.7 us
    all_gather x2, waiting for transfers between devices, reduce_rows(): part = lax.all_gather(part, 'x', axis=0, tiled=True)  66.3 us
    reduce_scatter x3, waiting for transfers between devices, reduce_rows(): part = lax.psum_scatter(part, 'x', scatter_dimension=0, tiled=True)  66.2 us
    reduce_scatter x3, waiting for transfers between devices, reduce_rows(): part = lax.psum_scatter(rows, 'c', scatter_dimension=0, tiled=True)  59.4 us
  transfers between devices with their start and end apart: 142, of which 69 were waited for; matrix products, arithmetic and copies ran while one was open for 12% of the time, Pallas kernels for 4%

profile of v1, /device:TPU:1, one launch (start us, length us, event | category | flops | bytes accessed | tf_op | source)
XLA Modules:
  0.0 898.8 jit_solution(14092965363733476359)
XLA Ops:
  57.7 11.7 %collective-permute-done.5 = bf16[32,2048]{1,0:T(8,128)(2,1)S(1)} collective-permute-done((bf16[32,2048]{1,0:T(8,128)(2,1)S(1)}, bf16[32,2048]{1,0:T(8,128)(2,1)S(1)}, u32[]{:S(2)}, u32[]{:S(2)}) %collective-permute-start.5) | collective-permute-done | bytes 131104 | tf_op jit(solution)/shard_map/ppermute | solution.py:379
  79.9 9.9 %mixer_fwd.2 = (bf16[512,256]{1,0:T(8,128)(2,1)S(1)}, f32[16,64,128]{2,1,0:T(8,128)S(1)}, f32[16,64,128]{2,1,0:T(8,128)S(1)}, f32[16,64,64]{2,1,0:T(8,128)S(1)},...) custom-call(s32[8]{0:T(128)S(1)} %fusion.66.slots, ...), custom_call_target="tpu_custom_call" | custom-call | tf_op jit(solution)/shard_map/mixer_fwd/pallas_call | solution.py:335
  100.3 9.9 %mixer_fwd.3 = (bf16[512,256]{1,0:T(8,128)(2,1)S(1)}, f32[16,64,128]{2,1,0:T(8,128)S(1)}, f32[16,64,128]{2,1,0:T(8,128)S(1)}, f32[16,64,64]{2,1,0:T(8,128)S(1)},...) custom-call(s32[8]{0:T(128)S(1)} %fusion.66.slots, ...), custom_call_target="tpu_custom_call" | custom-call | tf_op jit(solution)/shard_map/mixer_fwd/pallas_call | solution.py:335
  165.8 6.6 collective-permute-done.21
  203.8 6.5 collective-permute-done.73
  260.3 11.8 %collective-permute-done.53 = bf16[32,2048]{1,0:T(8,128)(2,1)S(1)} collective-permute-done((bf16[32,2048]{1,0:T(8,128)(2,1)S(1)}, bf16[32,2048]{1,0:T(8,128)(2,1)S(1)}, u32[]{:S(2)}, u32[]{:S(2)}) %collective-permute-start.53) | collective-permute-done | bytes 131104 | tf_op jit(solution)/shard_map/ppermute | solution.py:379
  341.3 13.7 %mixer_bwd.2 = (bf16[512,1152]{1,0:T(8,128)(2,1)S(1)}, f32[3,4,256]{2,1,0:T(4,128)S(1)}, f32[8,128]{1,0:T(8,128)S(1)}) custom-call(s32[8]{0:T(128)S(1)} %fusion.66.slots, f32[512,1152]{1,0:T(8,128)} %fusion.75.mixed_ref, f32[3,4,256]{2,1,0:T(4,128)S(1)} %copy-done.2, f32[2,128]{1,0:T(2,128)S(1)} %select_maximum_fusion.dec_ref, f32[1,128]{1,0:T(1,128)S(1)} %bitcast.154, ...), custom_call_target="tpu_custom_call" | custom-call | tf_op jit(solution)/shard_map/mixer_bwd/pallas_call | solution.py:335
  371.0 13.7 %mixer_bwd.3 = (bf16[512,1152]{1,0:T(8,128)(2,1)S(1)}, f32[3,4,256]{2,1,0:T(4,128)S(1)}, f32[8,128]{1,0:T(8,128)S(1)}) custom-call(s32[8]{0:T(128)S(1)} %fusion.66.slots, f32[512,1152]{1,0:T(8,128)} %fusion.73.mixed_ref, f32[3,4,256]{2,1,0:T(4,128)S(1)} %copy-done.2, f32[2,128]{1,0:T(2,128)S(1)} %select_maximum_fusion.dec_ref, f32[1,128]{1,0:T(1,128)S(1)} %bitcast.155, ...), custom_call_target="tpu_custom_call" | custom-call | tf_op jit(solution)/shard_map/mixer_bwd/pallas_call | solution.py:335
  393.2 6.0 slice.785
  420.3 20.0 %reduce-scatter.7.cloned.1.call-done = bf16[1024,1024]{0,1:T(8,128)(2,1)} async-done(((bf16[2048,1024]{0,1:T(8,128)(2,1)}), bf16[1024,1024]{0,1:T(8,128)(2,1)}) %reduce-scatter.7.cloned.1.call-update) | async-done | bytes 2097168 | tf_op jit(solution)/shard_map/reduce_scatter | solution.py:438
  440.4 23.7 %reduce-scatter.15.cloned.1.call-done = bf16[1056,2048]{1,0:T(8,128)(2,1)} async-done(((bf16[2112,2048]{1,0:T(8,128)(2,1)}), bf16[1056,2048]{1,0:T(8,128)(2,1)}) %reduce-scatter.15.cloned.1.call-update) | async-done | bytes 4325392 | tf_op jit(solution)/shard_map/reduce_scatter | solution.py:438
  464.2 15.6 %reduce-scatter.11.cloned.1.call-done = bf16[128,2048]{1,0:T(8,128)(2,1)} async-done(((bf16[256,2048]{1,0:T(8,128)(2,1)}), bf16[128,2048]{1,0:T(8,128)(2,1)}) %reduce-scatter.11.cloned.1.call-update) | async-done | bytes 524304 | tf_op jit(solution)/shard_map/reduce_scatter | solution.py:438
  479.9 32.8 %reduce-scatter.9.cloned.1.call-done = bf16[256,1024]{0,1:T(8,128)(2,1)} async-done(((bf16[1024,1024]{0,1:T(8,128)(2,1)}), bf16[256,1024]{0,1:T(8,128)(2,1)}) %reduce-scatter.9.cloned.1.call-update) | async-done | bytes 524304 | tf_op jit(solution)/shard_map/reduce_scatter | solution.py:439
  515.4 11.9 %collective-permute-done.128 = bf16[256,1024]{0,1:T(8,128)(2,1)S(1)} collective-permute-done((bf16[256,1024]{0,1:T(8,128)(2,1)}, bf16[256,1024]{0,1:T(8,128)(2,1)S(1)}, u32[]{:S(2)}, u32[]{:S(2)}) %collective-permute-start.128) | collective-permute-done | bytes 524320 | tf_op jit(solution)/shard_map/ppermute | solution.py:440
  529.3 33.4 %reduce-scatter.17.cloned.1.call-done = bf16[264,2048]{1,0:T(8,128)(2,1)} async-done(((bf16[1056,2048]{1,0:T(8,128)(2,1)}), bf16[264,2048]{1,0:T(8,128)(2,1)}) %reduce-scatter.17.cloned.1.call-update) | async-done | bytes 1081360 | tf_op jit(solution)/shard_map/reduce_scatter | solution.py:439
  565.5 23.8 %collective-permute-done.130 = bf16[264,2048]{1,0:T(8,128)(2,1)S(1)} collective-permute-done((bf16[264,2048]{1,0:T(8,128)(2,1)}, bf16[264,2048]{1,0:T(8,128)(2,1)S(1)}, u32[]{:S(2)}, u32[]{:S(2)}) %collective-permute-start.130) | collective-permute-done | bytes 1081376 | tf_op jit(solution)/shard_map/ppermute | solution.py:440
  598.5 13.3 %all_gather.20 = bf16[128,2048]{1,0:T(8,128)(2,1)} all-gather(bf16[32,2048]{1,0:T(8,128)(2,1)S(1)} %add_convert_fusion.23), channel_id=1, replica_groups=mesh['x'=4,'yh'=2,'c'=2,'z'=4,'yl'=2] {'x'}, dimensions={0}, use_global_device_ids=true | all-gather | bytes 655360 | tf_op jit(solution)/shard_map/all_gather | solution.py:441
  611.9 12.9 %all-gather.6.cloned.1.call-done = bf16[1024,1024]{0,1:T(8,128)(2,1)} async-done(((bf16[256,1024]{0,1:T(8,128)(2,1)}), bf16[1024,1024]{0,1:T(8,128)(2,1)}) %all-gather.6.cloned.1.call-update) | async-done | bytes 2097168 | tf_op jit(solution)/shard_map/all_gather | solution.py:441
  624.9 53.4 %all-gather.12.cloned.1.call-done = bf16[1056,2048]{1,0:T(8,128)(2,1)} async-done(((bf16[264,2048]{1,0:T(8,128)(2,1)}), bf16[1056,2048]{1,0:T(8,128)(2,1)}) %all-gather.12.cloned.1.call-update) | async-done | bytes 4325392 | tf_op jit(solution)/shard_map/all_gather | solution.py:441
  715.6 69.3 %all-reduce.3 = (f32[2048,2,2]{0,2,1:T(2,128)}, f32[3,4,256]{2,1,0:T(4,128)}, f32[2,2]{1,0:T(2,128)S(1)}) all-reduce(f32[2048,2,2]{0,2,1:T(2,128)S(1)} %reshape.140, f32[3,4,256]{2,1,0:T(4,128)S(1)} %add.476, f32[2,2]{1,0:T(2,128)S(1)} %slice.547), channel_id=1, replica_groups=mesh['x'=4,'yh'=2,'c'=2,'z'=4,'yl'=2] {'x','yh','c'}, use_global_device_ids=true, to_apply=%region_13.14 | all-reduce | flops 11268 | bytes 90144 | tf_op jit(solution)/shard_map/psum | solution.py:521
  798.3 68.9 %all-reduce.2 = (f32[2048]{0:T(1024)}, f32[128]{0:T(128)}, f32[2048]{0:T(1024)}) all-reduce(f32[2048]{0:T(1024)S(1)} %add.473, f32[128]{0:T(128)S(1)} %slice_bitcast_fusion, f32[2048]{0:T(1024)S(1)} %add.480), channel_id=1, replica_groups=mesh['x'=4,'yh'=2,'c'=2,'z'=4,'yl'=2] {'x','yh','c','z','yl'}, use_global_device_ids=true, to_apply=%region_10.11 | all-reduce | flops 4224 | bytes 33792 | tf_op jit(solution)/shard_map/psum | solution.py:524
  872.5 7.8 copy.28
  880.3 5.4 slice.660
  886.0 6.0 slice.659
  (617 shorter events, 394.3 us)
Async XLA Ops:
  7.2 433.1 %reduce-scatter.7.cloned.1.call-start = ((), (), s32[]{:S(2)}) async-start(), calls=%async_computation.6 | async-start | bytes 6291456 | tf_op jit(solution)/shard_map/reduce_scatter | solution.py:438
  53.3 38.8 %collective-permute-start.39 = (bf16[64,2048]{1,0:T(8,128)(2,1)}, bf16[64,2048]{1,0:T(8,128)(2,1)S(1)}, u32[]{:S(2)}, u32[]{:S(2)}) collective-permute-start(bf16[64,2048]{1,0:T(8,128)(2,1)} %get-tuple-element.195), channel_id=1, source_target_pairs={{0,2},{2,4},{4,6},{6,0},{1,3},{3,5},{5,7},{7,1},{8,10},{10,12},{12... | collective-permute-start | bytes 786440 | tf_op jit(solution)/shard_map/ppermute | solution.py:379
  54.5 78.6 %collective-permute-start.70 = (bf16[32,2048]{1,0:T(8,128)(2,1)S(1)}, bf16[32,2048]{1,0:T(8,128)(2,1)}, u32[]{:S(2)}, u32[]{:S(2)}) collective-permute-start(bf16[32,2048]{1,0:T(8,128)(2,1)S(1)} %slice.606), channel_id=1, source_target_pairs={{0,6},{2,0},{4,2},{6,4},{1,7},{3,1},{5,3},{7,5},{8,14},{10,8},{12,... | collective-permute-start | bytes 393224 | tf_op jit(solution)/shard_map/ppermute | solution.py:383
  56.1 77.1 %collective-permute-start.69 = (bf16[32,2048]{1,0:T(8,128)(2,1)}, bf16[32,2048]{1,0:T(8,128)(2,1)}, u32[]{:S(2)}, u32[]{:S(2)}) collective-permute-start(bf16[32,2048]{1,0:T(8,128)(2,1)} %slice.605), channel_id=1, source_target_pairs={{0,2},{2,4},{4,6},{6,0},{1,3},{3,5},{5,7},{7,1},{8,10},{10,12},{12... | collective-permute-start | bytes 393224 | tf_op jit(solution)/shard_map/ppermute | solution.py:379
  253.0 71.7 %collective-permute-start.87 = (bf16[64,2048]{1,0:T(8,128)(2,1)S(1)}, bf16[64,2048]{1,0:T(8,128)(2,1)S(1)}, u32[]{:S(2)}, u32[]{:S(2)}) collective-permute-start(bf16[64,2048]{1,0:T(8,128)(2,1)S(1)} %get-tuple-element.88), channel_id=1, source_target_pairs={{0,2},{2,4},{4,6},{6,0},{1,3},{3,5},{5,7},{7,1},{8,10},{10,12},{12... | collective-permute-start | bytes 786440 | tf_op jit(solution)/shard_map/ppermute | solution.py:379
  253.9 36.0 %collective-permute-start.103 = (bf16[64,2048]{1,0:T(8,128)(2,1)S(1)}, bf16[64,2048]{1,0:T(8,128)(2,1)S(1)}, u32[]{:S(2)}, u32[]{:S(2)}) collective-permute-start(bf16[64,2048]{1,0:T(8,128)(2,1)S(1)} %get-tuple-element.197), channel_id=1, source_target_pairs={{0,2},{2,4},{4,6},{6,0},{1,3},{3,5},{5,7},{7,1},{8,10},{10,12},{12... | collective-permute-start | bytes 786440 | tf_op jit(solution)/shard_map/ppermute | solution.py:379
  255.5 48.2 %collective-permute-start.86 = (bf16[32,2048]{1,0:T(8,128)(2,1)S(1)}, bf16[32,2048]{1,0:T(8,128)(2,1)S(1)}, u32[]{:S(2)}, u32[]{:S(2)}) collective-permute-start(bf16[32,2048]{1,0:T(8,128)(2,1)S(1)} %slice.619), channel_id=1, source_target_pairs={{0,6},{2,0},{4,2},{6,4},{1,7},{3,1},{5,3},{7,5},{8,14},{10,8},{12,... | collective-permute-start | bytes 393224 | tf_op jit(solution)/shard_map/ppermute | solution.py:383
  301.0 25.3 %collective-permute-start.59 = (bf16[64,2048]{1,0:T(8,128)(2,1)S(1)}, bf16[64,2048]{1,0:T(8,128)(2,1)S(1)}, u32[]{:S(2)}, u32[]{:S(2)}) collective-permute-start(bf16[64,2048]{1,0:T(8,128)(2,1)S(1)} %get-tuple-element.180), channel_id=1, source_target_pairs={{0,6},{2,0},{4,2},{6,4},{1,7},{3,1},{5,3},{7,5},{8,14},{10,8},{12,... | collective-permute-start | bytes 786440 | tf_op jit(solution)/shard_map/ppermute | solution.py:383
  399.3 64.8 %reduce-scatter.15.cloned.1.call-start = ((), (), s32[]{:S(2)}) async-start(), calls=%async_computation.13 | async-start | bytes 12976128 | tf_op jit(solution)/shard_map/reduce_scatter | solution.py:438
  415.8 64.0 %reduce-scatter.11.cloned.1.call-start = ((), (), s32[]{:S(2)}) async-start(), calls=%async_computation.10 | async-start | bytes 1572864 | tf_op jit(solution)/shard_map/reduce_scatter | solution.py:438
  420.3 92.4 %reduce-scatter.9.cloned.1.call-start = ((), (), s32[]{:S(2)}) async-start(), calls=%async_computation.7 | async-start | bytes 2621440 | tf_op jit(solution)/shard_map/reduce_scatter | solution.py:439
  440.3 122.4 %reduce-scatter.17.cloned.1.call-start = ((), (), s32[]{:S(2)}) async-start(), calls=%async_computation.14 | async-start | bytes 5406720 | tf_op jit(solution)/shard_map/reduce_scatter | solution.py:439
  464.1 127.8 %reduce-scatter.13.cloned.1.call-start = ((), (), s32[]{:S(2)}) async-start(), calls=%async_computation.11 | async-start | bytes 655360 | tf_op jit(solution)/shard_map/reduce_scatter | solution.py:439
  479.8 145.0 %all-gather.6.cloned.1.call-start = ((), (), s32[]{:S(2)}) async-start(), calls=%async_computation.8 | async-start | bytes 2621440 | tf_op jit(solution)/shard_map/all_gather | solution.py:441
  529.3 149.0 %all-gather.12.cloned.1.call-start = ((), (), s32[]{:S(2)}) async-start(), calls=%async_computation.15 | async-start | bytes 5406720 | tf_op jit(solution)/shard_map/all_gather | solution.py:441
  562.7 26.5 %collective-permute-start.130 = (bf16[264,2048]{1,0:T(8,128)(2,1)}, bf16[264,2048]{1,0:T(8,128)(2,1)S(1)}, u32[]{:S(2)}, u32[]{:S(2)}) collective-permute-start(bf16[264,2048]{1,0:T(8,128)(2,1)} %reduce-scatter.17.cloned.1.call-done), channel_id=1, source_target_pairs={{0,16},{16,0},{1,17},{17,1},{2,18},{18,2},{3,19},{19,3},{4,20},{20... | collective-permute-start | bytes 3244040 | tf_op jit(solution)/shard_map/ppermute | solution.py:440
  591.9 277.8 %all-gather.10.cloned.1.call-start = ((), (), s32[]{:S(2)}) async-start(), calls=%async_computation.12 | async-start | bytes 1572864 | tf_op jit(solution)/shard_map/all_gather | solution.py:442
  611.8 260.6 %all-gather.8.cloned.1.call-start = ((), (), s32[]{:S(2)}) async-start(), calls=%async_computation.9 | async-start | bytes 6291456 | tf_op jit(solution)/shard_map/all_gather | solution.py:442
  624.8 255.4 %all-gather.14.cloned.1.call-start = ((), (), s32[]{:S(2)}) async-start(), calls=%async_computation.16 | async-start | bytes 12976128 | tf_op jit(solution)/shard_map/all_gather | solution.py:442
  694.3 95.1 %collective-permute-start.91 = (bf16[64,2048]{1,0:T(8,128)(2,1)}, bf16[64,2048]{1,0:T(8,128)(2,1)S(1)}, u32[]{:S(2)}, u32[]{:S(2)}) collective-permute-start(bf16[64,2048]{1,0:T(8,128)(2,1)} %get-tuple-element.130), channel_id=1, source_target_pairs={{0,6},{2,0},{4,2},{6,4},{1,7},{3,1},{5,3},{7,5},{8,14},{10,8},{12,... | collective-permute-start | bytes 786440 | tf_op jit(solution)/shard_map/ppermute | solution.py:383
  700.2 89.7 %collective-permute-start.90 = (bf16[64,2048]{1,0:T(8,128)(2,1)}, bf16[64,2048]{1,0:T(8,128)(2,1)S(1)}, u32[]{:S(2)}, u32[]{:S(2)}) collective-permute-start(bf16[64,2048]{1,0:T(8,128)(2,1)} %get-tuple-element.122), channel_id=1, source_target_pairs={{0,1},{1,0},{2,3},{3,2},{4,5},{5,4},{6,7},{7,6},{8,9},{9,8},{10,11... | collective-permute-start | bytes 786440 | tf_op jit(solution)/shard_map/ppermute | solution.py:387
  706.2 78.8 %collective-permute-start.124 = (bf16[64,2048]{1,0:T(8,128)(2,1)}, bf16[64,2048]{1,0:T(8,128)(2,1)S(1)}, u32[]{:S(2)}, u32[]{:S(2)}) collective-permute-start(bf16[64,2048]{1,0:T(8,128)(2,1)} %get-tuple-element.121), channel_id=1, source_target_pairs={{0,2},{2,4},{4,6},{6,0},{1,3},{3,5},{5,7},{7,1},{8,10},{10,12},{12... | collective-permute-start | bytes 786440 | tf_op jit(solution)/shard_map/ppermute | solution.py:379
  710.5 75.1 %collective-permute-start.126 = (bf16[64,2048]{1,0:T(8,128)(2,1)S(1)}, bf16[64,2048]{1,0:T(8,128)(2,1)S(1)}, u32[]{:S(2)}, u32[]{:S(2)}) collective-permute-start(bf16[64,2048]{1,0:T(8,128)(2,1)S(1)} %pad_maximum_fusion.16), channel_id=1, source_target_pairs={{0,1},{1,0},{2,3},{3,2},{4,5},{5,4},{6,7},{7,6},{8,9},{9,8},{10,11... | collective-permute-start | bytes 786440 | tf_op jit(solution)/shard_map/ppermute | solution.py:387
  712.5 75.4 %collective-permute-start.121 = (bf16[64,2048]{1,0:T(8,128)(2,1)}, bf16[64,2048]{1,0:T(8,128)(2,1)}, u32[]{:S(2)}, u32[]{:S(2)}) collective-permute-start(bf16[64,2048]{1,0:T(8,128)(2,1)} %pad_maximum_fusion.15), channel_id=1, source_target_pairs={{0,6},{2,0},{4,2},{6,4},{1,7},{3,1},{5,3},{7,5},{8,14},{10,8},{12,... | collective-permute-start | bytes 786440 | tf_op jit(solution)/shard_map/ppermute | solution.py:383
  (185 other events, 2567.7 us)
Sparse Core Ops, SparseCore 0:
  399.4 40.8 reduce-scatter.6
  442.9 21.2 reduce-scatter.14
  467.2 12.6 reduce-scatter.10
  482.1 30.5 reduce-scatter.8
  515.1 47.5 reduce-scatter.16
  565.1 19.6 reduce-scatter.12
  587.1 37.6 all-gather.5
  627.2 51.1 all-gather.11
  680.1 12.5 all-gather.9
  694.2 17.6 all-gather.7
  713.8 24.9 all-gather.13

commit v2 on v1

--- a/solution.py
+++ b/solution.py
@@ -133,22 +133,38 @@
     return lax.rsqrt(jnp.sum(v * v, -1, keepdims=True) + EPS)
 
 
-def in_order(slots, source, target):
+def place(slots, n):
+    first = (slots[n] * pl.num_programs(0) + pl.program_id(0)) * BLOCK
+    return pl.ds(pl.multiple_of(first, BLOCK), BLOCK)
+
+
+def in_order(slots, pieces, held, target):
+    @pl.when(pl.program_id(0) == 0)
+    def _():
+        first = 0
+        for piece in pieces:
+            held[first : first + piece.shape[0], :] = piece[...]
+            first += piece.shape[0]
+
     for n in range(target.shape[0] // BLOCK):
-        target[n * BLOCK : (n + 1) * BLOCK, :] = source[pl.ds(pl.multiple_of(slots[n] * BLOCK, BLOCK), BLOCK), :]
-
-
-def to_slots(slots, rows, target, lanes):
-    for n in range(rows.shape[0] // BLOCK):
-        target[pl.ds(pl.multiple_of(slots[n] * BLOCK, BLOCK), BLOCK), lanes] = rows[n * BLOCK : (n + 1) * BLOCK]
-
-
-def fwd_kernel(
-    slots, mixed_ref, conv_ref, dec_ref, gain_ref,
-    rows_ref, out_ref, err_ref, inv_ref, sk_ref, state_ref, step_ref, proj_ref,
-):
+        target[n * BLOCK : (n + 1) * BLOCK, :] = held[place(slots, n), :]
+
+
+def out_slots(held, outs):
+    @pl.when(pl.program_id(0) == pl.num_programs(0) - 1)
+    def _():
+        size = outs[0].shape[0]
+        for i, out in enumerate(outs):
+            out[...] = held[i * size : (i + 1) * size, :]
+
+
+def fwd_kernel(slots, *refs):
+    pieces, refs = refs[:9], refs[9:]
+    w_ref, conv_ref, dec_ref, gain_ref, out_w_ref, *sums, normed_ref, proj_ref, rows_ref = refs[:16]
+    out_ref, err_ref, inv_ref, sk_ref, state_ref, step_ref, held_ref = refs[16:]
     width = WIDTH
-    in_order(slots, mixed_ref, proj_ref)
+    in_order(slots, pieces, held_ref, normed_ref)
+    proj_ref[...] = dot2(normed_ref[...], w_ref[...], 1, 0, None)
     _, _, act_q = activate(proj_ref[:, 0:width], conv_ref[0])
     _, _, act_k = activate(proj_ref[:, width : 2 * width], conv_ref[1])
     _, _, act_v = activate(proj_ref[:, 2 * width : 3 * width], conv_ref[2])
@@ -190,7 +206,11 @@
     scale = lax.rsqrt(jnp.mean(outputs * outputs, -1, keepdims=True) + EPS)
     gate = proj_ref[:, 3 * width : 4 * width]
     rows = (join_heads(outputs * scale * gain_ref[...]) * (gate * sigmoid(gate))).astype(jnp.bfloat16)
-    to_slots(slots, rows, rows_ref, slice(0, width))
+    rows_ref[...] = rows
+    product = dot2(rows, out_w_ref[...], 1, 0, None).astype(jnp.bfloat16)
+    for n in range(blocks):
+        held_ref[place(slots, n), :] = product[n * BLOCK : (n + 1) * BLOCK]
+    out_slots(held_ref, sums)
 
 
 def unit_back(act, d_norm, factor):
@@ -198,14 +218,13 @@
     return factor * (r * d_norm - act * (r * r * r) * jnp.sum(d_norm * act, -1, keepdims=True))
 
 
-def bwd_kernel(
-    slots, mixed_ref, conv_ref, dec_ref, gain_ref, drows_mixed_ref,
-    out_ref, err_ref, inv_ref, sk_ref, state_ref, step_ref,
-    dproj_ref, dconv_ref, dsmall_ref, proj_ref, drows_ref,
-):
+def bwd_kernel(slots, *refs):
+    pieces, refs = refs[:9], refs[9:]
+    proj_ref, conv_ref, dec_ref, gain_ref, out_w_ref, out_ref, err_ref, inv_ref, sk_ref, state_ref, step_ref = refs[:11]
+    grad_ref, dproj_ref, dconv_ref, dsmall_ref, held_ref = refs[11:]
     width = WIDTH
-    in_order(slots, mixed_ref, proj_ref)
-    in_order(slots, drows_mixed_ref, drows_ref)
+    in_order(slots, pieces, held_ref, grad_ref)
+    d_rows = dot2(grad_ref[...], out_w_ref[...], 1, 1, None)
     n = err_ref.shape[0]
     blocks = n // HEADS
     rates = proj_ref[:, 4 * width :]
@@ -226,13 +245,12 @@
 
     gate = proj_ref[:, 3 * width : 4 * width]
     sig_g = sigmoid(gate)
-    d_rows = drows_ref[...]
     scale = lax.rsqrt(jnp.mean(outputs * outputs, -1, keepdims=True) + EPS)
     gain = gain_ref[...]
     normal = outputs * scale
     d_gained = split_heads(d_rows * (gate * sig_g))
     d_gate = d_rows * join_heads(normal * gain) * (sig_g * (1.0 + gate * (1.0 - sig_g)))
-    to_slots(slots, d_gate.astype(jnp.bfloat16), dproj_ref, slice(3 * width, 4 * width))
+    dproj_ref[:, 3 * width : 4 * width] = d_gate.astype(jnp.bfloat16)
     d_gain = jnp.sum((d_gained * normal).reshape(n * BLOCK, HS), 0, keepdims=True)
     d_normal = d_gained * gain
     d_out = scale * d_normal - outputs * (scale * scale * scale) * jnp.mean(d_normal * outputs, -1, keepdims=True)
@@ -292,7 +310,7 @@
     decay_rate, decay_bias = dec_ref[0:1, :], dec_ref[1:2, :]
     d_first = d_log * -decay_rate * sigmoid(rates + decay_bias)
     d_rates = (d_first + d_update * update * (1.0 - update)).astype(jnp.bfloat16)
-    to_slots(slots, d_rates, dproj_ref, slice(4 * width, 4 * width + 128))
+    dproj_ref[:, 4 * width :] = d_rates
     small = jnp.concatenate(
         [
             jnp.sum(d_log * -soft, 0, keepdims=True),
@@ -322,51 +340,95 @@
             d_in = d_in + shift_up(d_pre, 3 - j) * taps[j : j + 1, :]
             sums.append(jnp.sum(d_pre * shift_down(rows, 3 - j), 0, keepdims=True))
         sums.append(jnp.sum(d_pre * rows, 0, keepdims=True))
-        to_slots(slots, d_in.astype(jnp.bfloat16), dproj_ref, slice(c * width, (c + 1) * width))
+        dproj_ref[:, c * width : (c + 1) * width] = d_in.astype(jnp.bfloat16)
         dconv_ref[c] = jnp.concatenate(sums, axis=0)
 
 
 def whole(shape):
-    return pl.BlockSpec(tuple(shape), lambda i, slots: (0,) * len(shape))
-
-
-def kernel_call(kernel, name, outs, ins, scratch):
+    return pl.BlockSpec(tuple(shape), lambda i, slots: (0,) * len(shape), pipeline_mode=pl.Buffered(1))
+
+
+def each(shape):
+    return pl.BlockSpec((None,) + tuple(shape[1:]), lambda i, slots: (i,) + (0,) * (len(shape) - 1))
+
+
+def kernel_call(kernel, name, micros, outs, ins, held, time):
     slots, rest = ins[0], ins[1:]
+    spec = lambda a: each(a.shape) if len(a.shape) > 2 and a.shape[0] == micros else whole(a.shape)
     return pl.pallas_call(
         kernel,
         grid_spec=pltpu.PrefetchScalarGridSpec(
             num_scalar_prefetch=1,
-            grid=(1,),
-            in_specs=[whole(a.shape) for a in rest],
-            out_specs=[whole(o.shape) for o in outs],
-            scratch_shapes=[pltpu.VMEM(shape, F32) for shape in scratch],
+            grid=(micros,),
+            in_specs=[spec(a) for a in rest],
+            out_specs=[spec(o) for o in outs],
+            scratch_shapes=[pltpu.VMEM(held, jnp.bfloat16)],
         ),
         out_shape=outs,
-        compiler_params=pltpu.CompilerParams(vmem_limit_bytes=48 * 2**20),
+        compiler_params=pltpu.CompilerParams(vmem_limit_bytes=62 * 2**20),
+        cost_estimate=cost(time),
         name=name,
     )(slots, *rest)
 
 
-def mixer_fwd(slots, mixed, conv, dec, gain):
-    positions = mixed.shape[0]
-    n = HEADS * positions // BLOCK
-    outs = [jax.ShapeDtypeStruct((positions, WIDTH), jnp.bfloat16)] + [
-        jax.ShapeDtypeStruct(shape, F32)
-        for shape in (
-            (n, BLOCK, HS), (n, BLOCK, HS), (n, BLOCK, BLOCK), (n, BLOCK, HS), (n, HS, HS), (n, HS, HS),
-        )
+def mixer_fwd(slots, pieces, w_in, conv, dec, gain, out_proj, micros):
+    rows, features = 8 * pieces[0].shape[0], pieces[0].shape[1]
+    own = rows // micros
+    n = HEADS * own // BLOCK
+    low = lambda *shape: jax.ShapeDtypeStruct(shape, jnp.bfloat16)
+    wide = lambda *shape: jax.ShapeDtypeStruct((micros,) + shape, F32)
+    outs = [low(rows // 8, features)] * 8
+    outs += [low(micros, own, features), wide(own, w_in.shape[1]), low(micros, own, WIDTH)]
+    outs += [wide(n, BLOCK, HS), wide(n, BLOCK, HS), wide(n, BLOCK, BLOCK), wide(n, BLOCK, HS)]
+    outs += [wide(n, HS, HS), wide(n, HS, HS)]
+    ins = (slots, *pieces, w_in, conv, dec, gain, out_proj)
+    done = kernel_call(fwd_kernel, "mixer_fwd", micros, outs, ins, (rows, features), 30)
+    return done[:8], done[8:11], done[11:]
+
+
+def mixer_bwd(slots, pieces, mixed, conv, dec, gain, out_proj, saved, micros):
+    rows, features = 8 * pieces[0].shape[0], pieces[0].shape[1]
+    outs = [
+        jax.ShapeDtypeStruct((micros, rows // micros, features), jnp.bfloat16),
+        jax.ShapeDtypeStruct(mixed.shape, jnp.bfloat16),
+        jax.ShapeDtypeStruct((micros,) + conv.shape, F32),
+        jax.ShapeDtypeStruct((micros, 8, 128), F32),
     ]
-    return kernel_call(fwd_kernel, "mixer_fwd", outs, (slots, mixed, conv, dec, gain), [mixed.shape])
-
-
-def mixer_bwd(slots, mixed, conv, dec, gain, d_rows, saved):
-    outs = [
-        jax.ShapeDtypeStruct(mixed.shape, jnp.bfloat16),
-        jax.ShapeDtypeStruct(conv.shape, F32),
-        jax.ShapeDtypeStruct((8, 128), F32),
-    ]
-    ins = (slots, mixed, conv, dec, gain, d_rows, *saved)
-    return kernel_call(bwd_kernel, "mixer_bwd", outs, ins, [mixed.shape, d_rows.shape])
+    ins = (slots, *pieces, mixed, conv, dec, gain, out_proj, *saved)
+    return kernel_call(bwd_kernel, "mixer_bwd", micros, outs, ins, (rows, features), 32)
+
+
+def normed_kernel(slots, d_ref, w_ref, *refs):
+    outs, held = refs[:-1], refs[-1]
+    micros, blocks, size, _ = d_ref.shape
+    for n in range(blocks):
+        for m in range(micros):
+            first = pl.multiple_of((slots[n] * micros + m) * size, size)
+            held[pl.ds(first, size), :] = d_ref[m, n]
+    product = dot2(held[...], w_ref[...], 1, 1, None).astype(jnp.bfloat16)
+    for i, out in enumerate(outs):
+        out[...] = product[i * size * micros : (i + 1) * size * micros]
+
+
+def normed_grad(slots, d_mixed, w_in):
+    micros, own, width = d_mixed.shape
+    slot = jax.ShapeDtypeStruct((micros * own // 8, w_in.shape[0]), jnp.bfloat16)
+    shape = (micros, 8, own // 8, width)
+    spec = lambda shape: pl.BlockSpec(tuple(shape), lambda i, slots: (0,) * len(shape))
+    return pl.pallas_call(
+        normed_kernel,
+        grid_spec=pltpu.PrefetchScalarGridSpec(
+            num_scalar_prefetch=1,
+            grid=(1,),
+            in_specs=[spec(shape), spec(w_in.shape)],
+            out_specs=[spec(slot.shape)] * 8,
+            scratch_shapes=[pltpu.VMEM((micros * own, width), jnp.bfloat16)],
+        ),
+        out_shape=[slot] * 8,
+        compiler_params=pltpu.CompilerParams(vmem_limit_bytes=48 * 2**20),
+        cost_estimate=cost(8),
+        name="normed_grad",
+    )(slots, d_mixed.reshape(shape), w_in)
 
 
 UP = [(i, (i + 1) % 4) for i in range(4)]
@@ -387,16 +449,17 @@
     return lax.ppermute(a, "yl", SWAP)
 
 
-def cuts(rows):
-    first = (rows // 3 + 15) // 16 * 16
-    return first, 2 * first
-
-
-def gather(own):
-    s, t = cuts(own.shape[0])
-    b0, am, ap = across(own), up(own), down(own)
-    bm, a2, bp = up(b0), down(ap), across(ap)
-    return jnp.concatenate([own, b0, ap, bp, a2, up(bm[:s]), down(bp[s:t]), across(a2[t:]), am, bm], axis=0)
+def phase(*arrays):
+    return lax.optimization_barrier(arrays)
+
+
+def gather(own, aside=None, needed=None):
+    half = own.shape[0] // 2
+    b0, am, ap = phase(across(own), up(own), down(own))
+    bm, a2, bp, needed = phase(up(b0), down(ap), across(ap), needed(b0) if needed else ())
+    other = [] if aside is None else [across(after(aside, bm))]
+    low, high, *other = phase(up(bm[:half]), down(bp[half:]), *other)
+    return [own, b0, ap, bp, a2, low, high, am, bm], other, needed
 
 
 def add(*parts):
@@ -406,17 +469,25 @@
     return total
 
 
-def scatter(whole):
-    rows = whole.shape[0] // 8
-    s, t = cuts(rows)
-    a0, b0, ap, bp, a2, b2, am, bm = (whole[i * rows : (i + 1) * rows] for i in range(8))
-    r1, r2, r3 = down(b2[:s]), up(b2[s:t]), across(b2[t:])
-    bm = jnp.concatenate([add(bm[:s], r1).astype(LOWP), bm[s:]], axis=0)
-    bp = jnp.concatenate([bp[:s], add(bp[s:t], r2).astype(LOWP), bp[t:]], axis=0)
-    a2 = jnp.concatenate([a2[:t], add(a2[t:], r3).astype(LOWP)], axis=0)
-    q1, q2, q3 = down(bm), up(a2), across(bp)
-    b0, ap = add(b0, q1).astype(LOWP), add(ap, q2, q3).astype(LOWP)
-    return add(a0, across(b0), down(am), up(ap))
+def scatter(*lists, one=(), two=None, late=None):
+    half = lists[0][0].shape[0] // 2
+    steps = [(down(b2[:half]), up(b2[half:])) for _, _, _, _, _, b2, _, _ in lists]
+    steps, one = phase(steps, one)
+    held = []
+    for (a0, b0, ap, bp, a2, _, am, bm), (r1, r2) in zip(lists, steps):
+        bm = jnp.concatenate([add(bm[:half], r1).astype(LOWP), bm[half:]], axis=0)
+        bp = jnp.concatenate([bp[:half], add(bp[half:], r2).astype(LOWP)], axis=0)
+        held.append((a0, b0, ap, am, down(bm), up(a2), across(bp)))
+    if two:
+        held, one = phase(held, two(one))
+    else:
+        (held,) = phase(held)
+    sent = []
+    for a0, b0, ap, am, q1, q2, q3 in held:
+        b0, ap = add(b0, q1).astype(LOWP), add(ap, q2, q3).astype(LOWP)
+        sent.append((a0, across(b0), down(am), up(ap)))
+    sent, one = phase(sent, late(one) if late else one)
+    return [add(*parts) for parts in sent], one
 
 
 def dot(a, b, ca, cb):
@@ -434,12 +505,240 @@
     return d_values, d_gain
 
 
-def reduce_rows(rows):
-    part = lax.psum_scatter(rows, "c", scatter_dimension=0, tiled=True)
-    part = lax.psum_scatter(part, "x", scatter_dimension=0, tiled=True)
-    part = add(part, lax.ppermute(part, "yh", SWAP)).astype(LOWP)
-    part = lax.all_gather(part, "x", axis=0, tiled=True)
-    return lax.all_gather(part, "c", axis=0, tiled=True)
+def ffn_kernel(at, *refs):
+    pieces, (grad_ref, gate_w, up_w, down_w) = refs[:-17], refs[-17:-13]
+    rows_ref, inner_ref, slots_ref, dgu_ref = refs[-13:-9]
+    outs, total = refs[-9:-1], refs[-1]
+    step = pl.program_id(0)
+    quarter = grad_ref.shape[0] // 4
+
+    @pl.when(step == 0)
+    def _():
+        first = 0
+        for piece in pieces:
+            rows_ref[first : first + piece.shape[0], :] = piece[...]
+            first += piece.shape[0]
+
+    rows = rows_ref[...]
+    gate = dot(gate_w[...], rows, 1, 1)
+    lift = dot(up_w[...], rows, 1, 1)
+    for dz in range(4):
+        lanes = slice(dz * quarter, (dz + 1) * quarter)
+        place = pl.ds(pl.multiple_of(lax.rem(at[0] + dz, 4) * quarter, quarter), quarter)
+        d_inner = dot(down_w[...], grad_ref[place, :], 1, 1)
+        g, u = gate[:, lanes], lift[:, lanes]
+        sigma = sigmoid(g)
+        inner = (g * sigma * u).astype(LOWP)
+        inner_ref[:, place] = inner
+        slots_ref[:, lanes] = inner
+        dgu_ref[0, :, lanes] = (d_inner * u * sigma * (1.0 + g * (1.0 - sigma))).astype(LOWP)
+        dgu_ref[1, :, lanes] = (d_inner * g * sigma).astype(LOWP)
+    both = dgu_ref[...].reshape(-1, dgu_ref.shape[2])
+    weights = jnp.concatenate([gate_w[...], up_w[...]], axis=0)
+    part = dot(both, weights, 0, 0)
+
+    @pl.when(step == 0)
+    def _():
+        total[...] = part
+
+    @pl.when(step == pl.num_programs(0) - 1)
+    def _():
+        size = outs[0].shape[0]
+        done = total[...] + part
+        for i, out in enumerate(outs):
+            out[...] = done[i * size : (i + 1) * size].astype(LOWP)
+
+
+def cost(microseconds):
+    return pl.CostEstimate(flops=microseconds * 10**9, bytes_accessed=microseconds * 3 * 10**6, transcendentals=0)
+
+
+def ffn_back(at, pieces, grad_rows, gate_up, down_proj):
+    rows, features = grad_rows.shape
+    units = down_proj.shape[0]
+    tile = units // 2
+    full = lambda shape: pl.BlockSpec(tuple(shape), lambda i, at: (0,) * len(shape))
+    part = pl.BlockSpec((tile, features), lambda i, at: (i, 0))
+    gate, lift = (pl.BlockSpec((None, tile, features), lambda i, at, k=k: (k, i, 0)) for k in range(2))
+    lines = pl.BlockSpec((tile, rows), lambda i, at: (i, 0))
+    pair = pl.BlockSpec((2, tile, rows), lambda i, at: (0, i, 0))
+    slot = (rows // 8, features)
+    return pl.pallas_call(
+        ffn_kernel,
+        grid_spec=pltpu.PrefetchScalarGridSpec(
+            num_scalar_prefetch=1,
+            grid=(2,),
+            in_specs=[full(p.shape) for p in pieces] + [full(grad_rows.shape), gate, lift, part],
+            out_specs=[full(grad_rows.shape), lines, lines, pair] + [full(slot)] * 8,
+            scratch_shapes=[pltpu.VMEM((rows, features), F32)],
+        ),
+        out_shape=[jax.ShapeDtypeStruct(grad_rows.shape, LOWP)]
+        + [jax.ShapeDtypeStruct((units, rows), LOWP)] * 2
+        + [jax.ShapeDtypeStruct((2, units, rows), LOWP)]
+        + [jax.ShapeDtypeStruct(slot, LOWP)] * 8,
+        compiler_params=pltpu.CompilerParams(vmem_limit_bytes=60 * 2**20),
+        cost_estimate=cost(28),
+        name="ffn",
+    )(at, *pieces, grad_rows, gate_up, gate_up, down_proj)
+
+
+def ffn_grads_kernel(at, dgu_ref, inner_ref, rows_ref, grad_ref, *refs):
+    out_ref = refs[-1]
+    width = rows_ref.shape[1]
+    for first, value in ((0, dot(dgu_ref[...], rows_ref[...], 1, 0)), (width, dot(inner_ref[...], grad_ref[...], 1, 0))):
+        lanes = slice(first, first + value.shape[1])
+        for ref in refs[:-1]:
+            value = value + ref[:, lanes].astype(F32)
+        out_ref[:, lanes] = value.astype(LOWP)
+
+
+def ffn_grads(half, dgu, inner, rows, grad_rows, *came):
+    units, count = inner.shape
+    tile = units // 4
+    features = rows.shape[1]
+    out = pl.BlockSpec((tile, features + features // 2), lambda i, at: (i, 0))
+    return pl.pallas_call(
+        ffn_grads_kernel,
+        grid_spec=pltpu.PrefetchScalarGridSpec(
+            num_scalar_prefetch=1,
+            grid=(4,),
+            in_specs=[
+                pl.BlockSpec((None, tile, count), lambda i, at: (at[0], i, 0)),
+                pl.BlockSpec((tile, count), lambda i, at: (2 * at[0] + i % 2, 0)),
+                pl.BlockSpec(rows.shape, lambda i, at: (0, 0)),
+                pl.BlockSpec((count, features // 2), lambda i, at: (0, i // 2)),
+            ]
+            + [out] * len(came),
+            out_specs=out,
+        ),
+        out_shape=jax.ShapeDtypeStruct((units, features + features // 2), LOWP),
+        compiler_params=pltpu.CompilerParams(vmem_limit_bytes=48 * 2**20),
+        cost_estimate=cost(9),
+        name="ffn_grads",
+    )(half, dgu, inner, rows, grad_rows, *came)
+
+
+def place_ffn_kernel(where, own_ref, other_ref, two_ref, down_ref):
+    def write(ref):
+        width = two_ref.shape[1]
+        two_ref[...] = ref[:, :width].astype(F32)
+        down_ref[...] = ref[:, width:].astype(F32)
+
+    pl.when(pl.program_id(0) < 4)(lambda: write(own_ref))
+    pl.when(pl.program_id(0) >= 4)(lambda: write(other_ref))
+
+
+def place_ffn(where, own, other, units, features):
+    tile = units // 4
+    core = lambda i, at: (at[0] + i // 4) % 2
+    part = lambda i, at: i % 4
+    return pl.pallas_call(
+        place_ffn_kernel,
+        grid_spec=pltpu.PrefetchScalarGridSpec(
+            num_scalar_prefetch=1,
+            grid=(8,),
+            in_specs=[
+                pl.BlockSpec((tile, own.shape[1]), lambda i, at: (jnp.minimum(i, 3), 0)),
+                pl.BlockSpec((tile, own.shape[1]), lambda i, at: (jnp.maximum(i - 4, 0), 0)),
+            ],
+            out_specs=[
+                pl.BlockSpec((None, tile, features), lambda i, at: (core(i, at), part(i, at), 0)),
+                pl.BlockSpec((tile, features // 2), lambda i, at: (2 * core(i, at) + part(i, at) % 2, part(i, at) // 2)),
+            ],
+        ),
+        out_shape=[jax.ShapeDtypeStruct((2, units, features), F32), jax.ShapeDtypeStruct((units, features), F32)],
+        compiler_params=pltpu.CompilerParams(vmem_limit_bytes=32 * 2**20),
+        cost_estimate=cost(9),
+        name="place_ffn",
+    )(where, own, other)
+
+
+def grads_kernel(at, rows_ref, proj_ref, mixed_ref, attn_ref, *refs):
+    out_ref = refs[-1]
+    came = [ref[...].astype(F32) for ref in refs[:-1]]
+
+    def write(value, first):
+        for more in came:
+            value = value + more[first : first + value.shape[0]]
+        out_ref[first : first + value.shape[0], :] = value.astype(LOWP)
+
+    @pl.when(pl.program_id(0) < pl.num_programs(0) - 1)
+    def _():
+        write(dot(rows_ref[...], proj_ref[...], 0, 0), 0)
+
+    @pl.when(pl.program_id(0) == pl.num_programs(0) - 1)
+    def _():
+        value = dot(mixed_ref[...], attn_ref[...], 0, 0)
+        width = out_ref.shape[1]
+        for i in range(2):
+            write(value[:, i * width : (i + 1) * width], i * value.shape[0])
+
+
+def mixer_grads(half, rows, d_mixed, mixer_rows, grad_attn, *came):
+    features, width = rows.shape[1] // 2, 4 * WIDTH
+    tile, steps = 256, features // 256
+    heads = mixer_rows.shape[1] // 2
+    out = pl.BlockSpec((tile, width), lambda i, at: (i, 0))
+    return pl.pallas_call(
+        grads_kernel,
+        grid_spec=pltpu.PrefetchScalarGridSpec(
+            num_scalar_prefetch=1,
+            grid=(steps + 1,),
+            in_specs=[
+                pl.BlockSpec((rows.shape[0], tile), lambda i, at: (0, at[0] * steps + jnp.minimum(i, steps - 1))),
+                pl.BlockSpec((rows.shape[0], width), lambda i, at: (0, 0)),
+                pl.BlockSpec((rows.shape[0], heads), lambda i, at: (0, at[0])),
+                pl.BlockSpec(grad_attn.shape, lambda i, at: (0, 0)),
+            ]
+            + [out] * len(came),
+            out_specs=out,
+        ),
+        out_shape=jax.ShapeDtypeStruct((features + tile, width), LOWP),
+        compiler_params=pltpu.CompilerParams(vmem_limit_bytes=48 * 2**20),
+        cost_estimate=cost(6),
+        name="mixer_grads",
+    )(half, rows, d_mixed, mixer_rows, grad_attn, *came)
+
+
+def place_kernel(core, part_ref, *refs):
+    out_ref = refs[-1]
+    width = out_ref.shape[2]
+    for k in range(out_ref.shape[1]):
+        out_ref[:, k, :] = part_ref[:, k * width : (k + 1) * width].astype(F32)
+
+
+def place_rows(core, half, shape, *rest):
+    steps = 4
+    rows = shape[0] // 2 // steps
+    return pl.pallas_call(
+        place_kernel,
+        grid_spec=pltpu.PrefetchScalarGridSpec(
+            num_scalar_prefetch=1,
+            grid=(steps,),
+            in_specs=[pl.BlockSpec((rows, half.shape[1]), lambda i, at: (i, 0))] + [pl.BlockSpec(memory_space=pl.ANY)] * len(rest),
+            out_specs=pl.BlockSpec((rows,) + shape[1:], lambda i, at: (at[0] * steps + i, 0, 0)),
+        ),
+        out_shape=jax.ShapeDtypeStruct(shape, F32),
+        input_output_aliases={2: 0} if rest else {},
+        cost_estimate=cost(5),
+        name="place_rows",
+    )(core, half, *rest)
+
+
+def after(value, *others):
+    return lax.optimization_barrier((value, others))[0]
+
+
+def over_yh(part):
+    return add(part, lax.ppermute(part, "yh", SWAP)).astype(LOWP)
+
+
+def butterfly(value, axis, size):
+    step = 1
+    while step < size:
+        value = value + lax.ppermute(value, axis, [(i, i ^ step) for i in range(size)])
+        step *= 2
+    return value
 
 
 def shards(
@@ -447,97 +746,116 @@
     out_gain, out_proj, ffn_gain, gate_up, down_proj,
 ):
     rows = tokens.shape[2]
-    micros = range(tokens.shape[1])
+    micros = tokens.shape[1]
     z, yl = lax.axis_index("z"), lax.axis_index("yl")
     places = (2 * z + yl) * rows + jnp.arange(rows, dtype=jnp.int32)
     block = jnp.arange(8, dtype=jnp.int32)
     slots = 2 * ((block // 2 - z) % 4) + (block % 2 + yl) % 2
 
     width = mixer_in.shape[1] * mixer_in.shape[2]
-    rate_pad = jnp.pad(rate_proj.reshape(rate_proj.shape[0], 4), ((0, 0), (0, 124)))
-    w_in = jnp.concatenate([mixer_in.reshape(mixer_in.shape[0], width), rate_pad], axis=1)
-    hidden_units = down_proj.shape[0]
-    w_gate, w_up = gate_up[:, 0, :].T, gate_up[:, 1, :].T
+    both_in = gate_up.transpose(1, 2, 0)
     dec = jnp.pad(jnp.stack([decay_rate, decay_bias]), ((0, 0), (0, 126)))
     gain_row = out_gain[None]
 
-    source = [tokens[0, m].astype(F32) for m in micros]
-    valid = [(places < lengths[0, m]).astype(F32)[:, None] for m in micros]
-    scale_one = [rms(source[m]) for m in micros]
-    rows_one = [gather((source[m] * scale_one[m] * attn_gain).astype(LOWP)) for m in micros]
-    grad_out = [cotangent[0, m].astype(F32) * valid[m] for m in micros]
-    grad_rows = [gather(grad_out[m].astype(LOWP)) for m in micros]
-
-    mixed, saved, mixer_rows, hidden, scale_two, rows_two = [], [], [], [], [], []
-    for m in micros:
-        mixed.append(dot(rows_one[m], w_in, 1, 0))
-        out, *keep = mixer_fwd(slots, mixed[m], conv_weight, dec, gain_row)
-        mixer_rows.append(out)
-        saved.append(keep)
-        attended = scatter(dot(out, out_proj, 1, 0).astype(LOWP))
-        hidden.append(source[m] + attended)
-        scale_two.append(rms(hidden[m]))
-        rows_two.append(gather((hidden[m] * scale_two[m] * ffn_gain).astype(LOWP)))
-
-    layer_out, d_hidden, grad_attn = [], [], []
-    d_ffn_gain = 0.0
-    d_down, d_gate, d_up = 0.0, 0.0, 0.0
-    for m in micros:
-        gate = dot(w_gate, rows_two[m], 1, 1)
-        lift = dot(w_up, rows_two[m], 1, 1)
-        sigma = jax.nn.sigmoid(gate)
-        inner = (gate * sigma * lift).astype(LOWP)
-        branch = scatter(dot(inner, down_proj, 0, 0).astype(LOWP))
-        layer_out.append(((hidden[m] + branch) * valid[m]).astype(LOWP))
-        d_inner = dot(down_proj, grad_rows[m], 1, 1)
-        dg = (d_inner * lift * sigma * (1.0 + gate * (1.0 - sigma))).astype(LOWP)
-        du = (d_inner * gate * sigma).astype(LOWP)
-        d_normed = (dot(dg, w_gate, 0, 0) + dot(du, w_up, 0, 0)).astype(LOWP)
-        d_normed = scatter(d_normed)
-        d_down = d_down + dot(inner, grad_rows[m], 1, 0)
-        d_gate = d_gate + dot(dg, rows_two[m], 1, 0)
-        d_up = d_up + dot(du, rows_two[m], 1, 0)
-        d_from, part = norm_back(hidden[m], scale_two[m], ffn_gain, d_normed)
-        d_ffn_gain = d_ffn_gain + part
-        d_hidden.append(grad_out[m] + d_from)
-        grad_attn.append(gather(d_hidden[m].astype(LOWP)))
-    ffn = reduce_rows(jnp.concatenate([d_gate.astype(LOWP), d_up.astype(LOWP), d_down.astype(LOWP)], axis=0))
-
-    d_tokens = []
-    d_attn_gain, d_conv, d_small, d_out, d_in = 0.0, 0.0, 0.0, 0.0, 0.0
-    for m in micros:
-        d_out = d_out + dot(mixer_rows[m], grad_attn[m], 0, 0)
-        d_mixer_rows = dot(grad_attn[m], out_proj, 1, 1)
-        d_mixed, conv_part, small_part = mixer_bwd(slots, mixed[m], conv_weight, dec, gain_row, d_mixer_rows, saved[m])
-        d_normed = scatter(dot(d_mixed, w_in, 1, 1).astype(LOWP))
-        d_in = d_in + dot(rows_one[m], d_mixed, 0, 0)
-        d_conv, d_small = d_conv + conv_part, d_small + small_part
-        d_from, part = norm_back(source[m], scale_one[m], attn_gain, d_normed)
-        d_attn_gain = d_attn_gain + part
-        d_tokens.append((d_hidden[m] + d_from).astype(LOWP))
-    d_out = reduce_rows(d_out.astype(LOWP))
-    d_mixer_in = reduce_rows(d_in[:, :width].astype(LOWP))
-    dp = ("x", "yh", "c")
-    d_rate, d_conv, d_pair = lax.psum(
-        (d_in[:, width : width + 4], d_conv, d_small[:2, :2]), dp
-    )
-    d_attn_gain, d_ffn_gain, d_out_gain = lax.psum((d_attn_gain, d_ffn_gain, d_small[2]), dp + ("z", "yl"))
-    ffn = ffn.astype(F32)
-    d_gate_up = ffn[: 2 * hidden_units].reshape(2, hidden_units, -1).transpose(2, 0, 1)
+    source = tokens[0].astype(F32).reshape(-1, tokens.shape[3])
+    valid = jnp.concatenate([(places < lengths[0, m]).astype(F32)[:, None] for m in range(micros)], axis=0)
+    scale_one = rms(source)
+    grad_out = cotangent[0].astype(F32).reshape(source.shape) * valid
+    grad_low = grad_out.astype(LOWP)
+    swap = lambda a: lax.ppermute(a, "c", SWAP)
+    scatter_x = lambda a: lax.psum_scatter(a, "x", scatter_dimension=0, tiled=True)
+    core = lax.axis_index("c")
+
+    normed = (source * scale_one * attn_gain).astype(LOWP)
+
+    def weights(start):
+        parts, rates = after((mixer_in, rate_proj), start)
+        rates = jnp.pad(rates.reshape(rates.shape[0], 4), ((0, 0), (0, 124)))
+        return jnp.concatenate([parts.reshape(parts.shape[0], width), rates], axis=1)
+
+    pieces, (grad_other,), w_in = gather(normed, grad_low, weights)
+    pieces = after(pieces, grad_other)
+    grad_rows = lax.all_gather(jnp.concatenate([grad_low, grad_other], axis=0), "z", axis=0, tiled=True)
+
+    sums, (rows_one, mixed, mixer_rows), saved = mixer_fwd(
+        slots, pieces, w_in, conv_weight, dec, gain_row, out_proj, micros
+    )
+    (attended,), grad_rows = scatter(sums, two=lambda _: grad_rows)
+    hidden = source + attended
+    scale_two = rms(hidden)
+    pieces, _, _ = gather((hidden * scale_two * ffn_gain).astype(LOWP))
+
+    rows_two, inner, inner_slots, dgu, *parts = ffn_back(z[None], pieces, grad_rows, both_in, down_proj)
+    half_of = lambda core, inner, *came: ffn_grads(core[None], dgu, inner, rows_two, grad_rows, *came)
+    (d_normed,), d_ffn = scatter(
+        parts,
+        one=half_of(1 - core, inner),
+        two=swap,
+        late=lambda came: half_of(core, inner, came),
+    )
+    d_ffn = scatter_x(d_ffn)
+    d_from, d_ffn_gain = norm_back(hidden, scale_two, ffn_gain, d_normed)
+    d_hidden = grad_out + d_from
+    branch = dot(inner_slots, down_proj, 0, 0).astype(LOWP)
+    branch = [branch[i * source.shape[0] : (i + 1) * source.shape[0]] for i in range(8)]
+    pieces, _, branch = gather(d_hidden.astype(LOWP), None, lambda _: branch)
+    pieces, d_ffn = phase(pieces, d_ffn)
+    d_ffn = over_yh(d_ffn)
+
+    grad_attn, d_mixed, d_conv, d_small = mixer_bwd(
+        slots, pieces, mixed, conv_weight, dec, gain_row, out_proj, saved, micros
+    )
+    d_mixed, d_ffn = phase(d_mixed, d_ffn)
+    half_of = lambda core, *came: mixer_grads(
+        core[None], *(a.reshape(-1, a.shape[2]) for a in (rows_one, d_mixed, mixer_rows, grad_attn)), *came
+    )
+    d_ffn = lax.all_gather(d_ffn, "x", axis=0, tiled=True)
+    came, parts = phase(swap(half_of(1 - core)), normed_grad(slots, d_mixed, w_in))
+    (d_normed, branch), (d_ffn, d_in) = scatter(
+        parts,
+        branch,
+        one=half_of(core, came),
+        late=lambda d_in: ((d_ffn, swap(d_ffn)), scatter_x(after(d_in, d_ffn))),
+    )
+    layer_out = ((hidden + branch) * valid).astype(LOWP)
+    d_two, d_down = place_ffn(core[None], *d_ffn, dgu.shape[1], rows_two.shape[1])
+    across_yh, d_two, d_down, layer_out = phase(lax.ppermute(d_in, "yh", SWAP), d_two, d_down, layer_out)
+    d_in = lax.all_gather(add(d_in, across_yh).astype(LOWP), "x", axis=0, tiled=True)
+    d_rate = dot(d_mixed[:, :, width:].reshape(-1, 128), rows_one.reshape(-1, rows_one.shape[2]), 0, 0)[:4]
+    d_conv, d_small = d_conv.sum(0), d_small.sum(0)
+    d_from, d_attn_gain = norm_back(source, scale_one, attn_gain, d_normed)
+    d_tokens = (d_hidden + d_from).astype(LOWP)
+
+    flat = [d_rate, d_conv, d_small[:2], d_attn_gain, d_ffn_gain, d_small[2]]
+    sizes = [a.size for a in flat]
+    small = jnp.concatenate([a.reshape(-1) for a in flat]).reshape(-1, 128)
+    small = butterfly(butterfly(butterfly(small, "c", 2), "x", 4), "yh", 2)
+    own = small.reshape(-1)[: sum(sizes[:3])]
+    gains = butterfly(butterfly(small[sum(sizes[:3]) // 128 :], "yl", 2), "z", 4).reshape(-1)
+    d_rate = own[: sizes[0]].reshape(2, 2, -1).transpose(2, 0, 1)
+    d_conv = own[sizes[0] : sizes[0] + sizes[1]].reshape(conv_weight.shape)
+    d_pair = own[sizes[0] + sizes[1] :].reshape(2, 128)
+    d_in, d_rate, d_conv, d_pair, gains, d_tokens = phase(d_in, d_rate, d_conv, d_pair, gains, d_tokens)
+
+    other = swap(d_in)
+    d_mixer_in, other = phase(place_rows(core[None], d_in, mixer_in.shape), other)
+    d_mixer_in = place_rows(1 - core[None], other, mixer_in.shape, d_mixer_in)
+    d_out = [a[4 * WIDTH :].reshape(2, -1, 4 * WIDTH).transpose(1, 0, 2).reshape(-1, 8 * WIDTH) for a in (d_in, other)]
+    d_out = jnp.concatenate([jnp.where(core == 0, *d_out), jnp.where(core == 0, *d_out[::-1])], axis=0).astype(F32)
     return (
-        jnp.stack(layer_out)[None],
-        jnp.stack(d_tokens)[None],
-        d_attn_gain,
-        d_mixer_in.astype(F32).reshape(mixer_in.shape),
-        d_rate.reshape(rate_proj.shape),
+        layer_out.reshape(tokens.shape),
+        d_tokens.reshape(tokens.shape),
+        gains[: sizes[3]],
+        d_mixer_in,
+        d_rate,
         d_conv,
-        d_pair[0],
-        d_pair[1],
-        d_out_gain,
-        d_out.astype(F32),
-        d_ffn_gain,
-        d_gate_up,
-        ffn[2 * hidden_units :],
+        d_pair[0, :2],
+        d_pair[1, :2],
+        gains[sizes[3] + sizes[4] :],
+        d_out,
+        gains[sizes[3] : sizes[3] + sizes[4]],
+        d_two.transpose(2, 0, 1),
+        d_down,
     )
 
 

time: 907 us -> 532 us (0.59)
  waiting for transfers between devices: 403 us -> 185 us
  blocking collectives: 152 us -> 0 us
  Pallas kernels: 47.1 us -> 153 us
  matrix products: 66.7 us -> 6.77 us
  starting transfers between devices: 125 us -> 91.3 us
  local copies, waits for them, and re-layouts: 53.4 us -> 33.6 us
    psum x2 -> x0, blocking collectives: 138 us -> none  [the longest x1 69.3 us: shards(): lax.psum((d_in[:, width:width + 4], d_conv, d_small[:2, :2]), dp)]
    reduce_scatter x6 -> x2, waiting for transfers between devices: 126 us -> 10.1 us  [shards(): lax.psum_scatter(a, 'x', scatter_dimension=0, tiled=True)]
    pallas_call x0 -> x9, Pallas kernels: none -> 88.7 us  [the longest x1 27.5 us: ffn_back(): pl.pallas_call(ffn_kernel, grid_spec=pltpu.PrefetchScalarGridSpec(num_sca...]
    dot_general x30 -> x2, matrix products: 66.7 us -> 6.77 us  [dot(): lax.dot_general(a, b, (((ca,), (cb,)), ((), ())), preferred_element_type=...]
    all_gather x5 -> x3, waiting for transfers between devices: 66.3 us -> 10.7 us  [the longest x1 8.45 us: shards(): d_ffn = lax.all_gather(d_ffn, 'x', axis=0, tiled=True)]
    ppermute x48 -> x21, waiting for transfers between devices: 55 us -> 20.8 us  [down(): return lax.ppermute(a, 'z', DOWN)]
    ppermute x48 -> x21, starting transfers between devices: 67.9 us -> 42.8 us  [down(): return lax.ppermute(a, 'z', DOWN)]
    ppermute x3 -> x13, starting transfers between devices: 8.31 us -> 27.3 us  [the longest x4 15.2 us: shards(): swap = lambda a: lax.ppermute(a, 'c', SWAP)]
  transfers between devices with their start and end apart: 142 -> 75, of which waited for: 69 -> 42; matrix products, arithmetic and copies ran while one was open for 12% -> 10% of each run, Pallas kernels for 4% -> 23%
where the time goes in v2:
time: 532 us; the launch traced here: 526 us
  waiting for transfers between devices  185 us (35%)
  Pallas kernels  153 us (29%)
  starting transfers between devices  91.3 us (17%)
  other arithmetic  41.4 us (8%)
  local copies, waits for them, and re-layouts  33.6 us (6%)
  between operations  15.2 us (3%)
  matrix products  6.77 us (1%)
    ppermute x21, waiting for transfers between devices, up(): return lax.ppermute(a, 'z', UP)  76.1 us
    pallas_call x2, Pallas kernels, kernel_call(): pl.pallas_call(kernel, grid_spec=pltpu.PrefetchScalarGridSpec(num_scalar_...  64 us
    ppermute x15, waiting for transfers between devices, across(): return lax.ppermute(a, 'yl', SWAP)  46.9 us
    ppermute x21, starting transfers between devices, down(): return lax.ppermute(a, 'z', DOWN)  42.8 us
    pallas_call x1, Pallas kernels, ffn_back(): pl.pallas_call(ffn_kernel, grid_spec=pltpu.PrefetchScalarGridSpec(num_sca...  27.5 us
    ppermute x21, waiting for transfers between devices, down(): return lax.ppermute(a, 'z', DOWN)  20.8 us
    ppermute x7, waiting for transfers between devices, butterfly(): lax.ppermute(value, axis, [(i, i ^ step) for i in range(size)])  20.7 us
    pallas_call x2, Pallas kernels, ffn_grads(): pl.pallas_call(ffn_grads_kernel, grid_spec=pltpu.PrefetchScalarGridSpec(n...  20.3 us
  transfers between devices with their start and end apart: 75, of which 42 were waited for; matrix products, arithmetic and copies ran while one was open for 10% of the time, Pallas kernels for 23%

profile of v2, /device:TPU:1, one launch (start us, length us, event | category | flops | bytes accessed | tf_op | source)
XLA Modules:
  0.0 526.3 jit_solution(11139322364747065220)
XLA Ops:
  36.7 5.4 %collective-permute-done.3.refs_8_ = bf16[128,2048]{1,0:T(8,128)(2,1)S(1)} collective-permute-done((bf16[128,2048]{1,0:T(8,128)(2,1)}, bf16[128,2048]{1,0:T(8,128)(2,1)S(1)}, u32[]{:S(2)}, u32[]{:S(2)}) %collective-permute-start.3) | collective-permute-done | bytes 524320 | tf_op jit(solution)/shard_map/ppermute | solution.py:441
  54.8 33.1 %mixer_fwd.1 = (bf16[128,2048]{1,0:T(8,128)(2,1)}, bf16[128,2048]{1,0:T(8,128)(2,1)}, bf16[128,2048]{1,0:T(8,128)(2,1)}, bf16[128,2048]{1,0:T(8,128)(2,1)}, bf16...) custom-call(s32[8]{0:T(128)} %fusion.16.slots, ...), custom_call_target="tpu_custom_call" | custom-call | flops 30000001024 | bytes 90000000 | tf_op jit(solution)/shard_map/mixer_fwd/pallas_call | solution.py:358
  92.7 8.9 %collective-permute-done.9 = bf16[64,2048]{1,0:T(8,128)(2,1)S(1)} collective-permute-done((bf16[64,2048]{1,0:T(8,128)(2,1)S(1)}, bf16[64,2048]{1,0:T(8,128)(2,1)S(1)}, u32[]{:S(2)}, u32[]{:S(2)}) %collective-permute-start.9) | collective-permute-done | bytes 262176 | tf_op jit(solution)/shard_map/ppermute | solution.py:445
  105.6 14.7 %collective-permute-done.12 = bf16[128,2048]{1,0:T(8,128)(2,1)S(1)} collective-permute-done((bf16[128,2048]{1,0:T(8,128)(2,1)}, bf16[128,2048]{1,0:T(8,128)(2,1)S(1)}, u32[]{:S(2)}, u32[]{:S(2)}) %collective-permute-start.12) | collective-permute-done | bytes 524320 | tf_op jit(solution)/shard_map/ppermute | solution.py:441
  124.6 7.1 %collective-permute-done.14 = bf16[128,2048]{1,0:T(8,128)(2,1)S(1)} collective-permute-done((bf16[128,2048]{1,0:T(8,128)(2,1)S(1)}, bf16[128,2048]{1,0:T(8,128)(2,1)S(1)}, u32[]{:S(2)}, u32[]{:S(2)}) %collective-permute-start.14) | collective-permute-done | bytes 524320 | tf_op jit(solution)/shard_map/ppermute | solution.py:449
  139.6 6.9 %collective-permute-done.17.refs_1_ = bf16[128,2048]{1,0:T(8,128)(2,1)S(1)} collective-permute-done((bf16[128,2048]{1,0:T(8,128)(2,1)S(1)}, bf16[128,2048]{1,0:T(8,128)(2,1)S(1)}, u32[]{:S(2)}, u32[]{:S(2)}) %collective-permute-start.17) | collective-permute-done | bytes 524320 | tf_op jit(solution)/shard_map/ppermute | solution.py:449
  152.3 6.2 %collective-permute-done.20.refs_8_ = bf16[128,2048]{1,0:T(8,128)(2,1)S(1)} collective-permute-done((bf16[128,2048]{1,0:T(8,128)(2,1)S(1)}, bf16[128,2048]{1,0:T(8,128)(2,1)S(1)}, u32[]{:S(2)}, u32[]{:S(2)}) %collective-permute-start.20) | collective-permute-done | bytes 524320 | tf_op jit(solution)/shard_map/ppermute | solution.py:441
  166.4 27.5 %ffn.1 = (bf16[1024,2048]{1,0:T(8,128)(2,1)}, bf16[704,1024]{1,0:T(8,128)(2,1)}, bf16[704,1024]{1,0:T(8,128)(2,1)}, bf16[2,704,1024]{2,1,0:T(8,128)(2,1)}, bf16[...) custom-call(s32[1]{0:T(128)} %bitcast.10.at, ...), custom_call_target="tpu_custom_call" | custom-call | flops 28000000000 | bytes 84000000 | tf_op jit(solution)/shard_map/ffn/pallas_call | solution.py:566
  201.3 9.9 %ffn_grads.2 = bf16[704,3072]{1,0:T(8,128)(2,1)} custom-call(s32[1]{0:T(128)} %bitcast.at, bf16[2,704,1024]{2,1,0:T(8,128)(2,1)S(1)} %copy-done.9, bf16[704,1024]{1,0:T(8,128)(2,1)S(1)} %copy-done.10, bf16[1024,2048]{1,0:T(8,128)(2,1)} %get-tuple-element.259.rows_ref, bf16[1024,2048]{1,0:T(8,128)(2,1)} %all-gather.4.cloned.1.call-done.refs_9_.grad_ref), custom_call_target="tpu_custom_call" | custom-call | flops 8999999488 | bytes 27000000 | tf_op jit(solution)/shard_map/ffn_grads/pallas_call | solution.py:600
  211.2 7.9 %collective-permute-start.30 = (bf16[704,3072]{1,0:T(8,128)(2,1)}, bf16[704,3072]{1,0:T(8,128)(2,1)S(1)}, u32[]{:S(2)}, u32[]{:S(2)}) collective-permute-start(bf16[704,3072]{1,0:T(8,128)(2,1)} %ffn_grads.2), channel_id=1, source_target_pairs={{0,8},{8,0},{1,9},{9,1},{2,10},{10,2},{3,11},{11,3},{4,12},{12,4},... | collective-permute-start | bytes 12976136 | tf_op jit(solution)/shard_map/ppermute | solution.py:765
  223.7 10.7 %collective-permute-done.28 = bf16[128,2048]{1,0:T(8,128)(2,1)S(1)} collective-permute-done((bf16[128,2048]{1,0:T(8,128)(2,1)S(1)}, bf16[128,2048]{1,0:T(8,128)(2,1)S(1)}, u32[]{:S(2)}, u32[]{:S(2)}) %collective-permute-start.28) | collective-permute-done | bytes 524320 | tf_op jit(solution)/shard_map/ppermute | solution.py:441
  240.6 10.4 %ffn_grads.3 = bf16[704,3072]{1,0:T(8,128)(2,1)} custom-call(s32[1]{0:T(128)} %bitcast.12.at.where.core, bf16[2,704,1024]{2,1,0:T(8,128)(2,1)S(1)} %copy-done.9, bf16[704,1024]{1,0:T(8,128)(2,1)S(1)} %copy-done.10, bf16[1024,2048]{1,0:T(8,128)(2,1)} %get-tuple-element.259.rows_ref, bf16[1024,2048]{1,0:T(8,128)(2,1)} %all-gather.4.cloned.1.call-done.refs_9_.grad_ref, ...), custom_call_target="tpu_custom_call" | custom-call | flops 8999999488 | bytes 27000000 | tf_op jit(solution)/shard_map/ffn_grads/pallas_call | solution.py:600
  275.8 8.2 %collective-permute-done.37.refs_8_ = bf16[128,2048]{1,0:T(8,128)(2,1)S(1)} collective-permute-done((bf16[128,2048]{1,0:T(8,128)(2,1)S(1)}, bf16[128,2048]{1,0:T(8,128)(2,1)S(1)}, u32[]{:S(2)}, u32[]{:S(2)}) %collective-permute-start.37) | collective-permute-done | bytes 524320 | tf_op jit(solution)/shard_map/ppermute | solution.py:441
  286.8 5.1 collective-permute-done.40.refs_5_
  291.9 10.1 %reduce-scatter.3.cloned.1.call-done = bf16[176,3072]{1,0:T(8,128)(2,1)} async-done(((bf16[704,3072]{1,0:T(8,128)(2,1)}), bf16[176,3072]{1,0:T(8,128)(2,1)}) %reduce-scatter.3.cloned.1.call-update) | async-done | bytes 1081360 | tf_op jit(solution)/shard_map/reduce_scatter | solution.py:766
  304.9 30.9 %mixer_bwd.1 = (bf16[2,512,2048]{2,1,0:T(8,128)(2,1)}, bf16[2,512,1152]{2,1,0:T(8,128)(2,1)}, f32[2,3,4,256]{3,2,1,0:T(4,128)}, f32[2,8,128]{2,1,0:T(8,128)}) custom-call(s32[8]{0:T(128)} %fusion.16.slots, bf16[128,2048]{1,0:T(8,128)(2,1)} %copy-done.32, bf16[128,2048]{1,0:T(8,128)(2,1)} %copy-done.69, bf16[128,2048]{1,0:T(8,128)(2,1)} %copy-done.71, ...), custom_call_target="tpu_custom_call" | custom-call | flops 32000000000 | bytes 96000000 | tf_op jit(solution)/shard_map/mixer_bwd/pallas_call | solution.py:358
  339.4 6.8 %mixer_grads.2 = bf16[1280,1024]{1,0:T(8,128)(2,1)S(1)} custom-call(s32[1]{0:T(128)} %bitcast.at, bf16[1024,2048]{1,0:T(8,128)(2,1)} %bitcast.95, bf16[1024,1152]{1,0:T(8,128)(2,1)S(1)} %bitcast.89, bf16[1024,256]{1,0:T(8,128)(2,1)S(1)} %bitcast.91, bf16[1024,2048]{1,0:T(8,128)(2,1)} %bitcast.115), custom_call_target="tpu_custom_call" | custom-call | flops 6000000000 | bytes 18000000 | tf_op jit(solution)/shard_map/mixer_grads/pallas_call | solution.py:682
  352.2 9.6 %normed_grad.1 = (bf16[128,2048]{1,0:T(8,128)(2,1)S(1)}, bf16[128,2048]{1,0:T(8,128)(2,1)S(1)}, bf16[128,2048]{1,0:T(8,128)(2,1)S(1)}, bf16[128,2048]{1,0:T(8,12...) custom-call(s32[8]{0:T(128)S(1)} %copy-done.8, ...), custom_call_target="tpu_custom_call" | custom-call | flops 8000000000 | bytes 24000000 | tf_op jit(solution)/shard_map/normed_grad/pallas_call | solution.py:418
  365.5 8.5 %mixer_grads.3 = bf16[1280,1024]{1,0:T(8,128)(2,1)} custom-call(s32[1]{0:T(128)} %bitcast.12.at.where.core, bf16[1024,2048]{1,0:T(8,128)(2,1)} %bitcast.96, bf16[1024,1152]{1,0:T(8,128)(2,1)S(1)} %bitcast.90, bf16[1024,256]{1,0:T(8,128)(2,1)S(1)} %bitcast.92, bf16[1024,2048]{1,0:T(8,128)(2,1)} %bitcast.116, bf16[1280,1024]{1,0:T(8,128)(2,1)} %copy-done.66), custom_call_target="tpu_custom_call" | custom-call | flops 6000000000 | bytes 18000000 | tf_op jit(solution)/shard_map/mixer_grads/pallas_call | solution.py:682
  378.0 8.4 %all-gather.6.cloned.1.call-done.own_ref = bf16[704,3072]{1,0:T(8,128)(2,1)} async-done(((bf16[176,3072]{1,0:T(8,128)(2,1)}), bf16[704,3072]{1,0:T(8,128)(2,1)}) %all-gather.6.cloned.1.call-update) | async-done | bytes 4325392 | tf_op jit(solution)/shard_map/all_gather | solution.py:812
  405.1 7.2 %collective-permute-done.51 = bf16[128,2048]{1,0:T(8,128)(2,1)S(1)} collective-permute-done((bf16[128,2048]{1,0:T(8,128)(2,1)S(1)}, bf16[128,2048]{1,0:T(8,128)(2,1)S(1)}, u32[]{:S(2)}, u32[]{:S(2)}) %collective-permute-start.51) | collective-permute-done | bytes 524320 | tf_op jit(solution)/shard_map/ppermute | solution.py:445
  422.6 5.6 %collective-permute-done.54 = bf16[128,2048]{1,0:T(8,128)(2,1)S(1)} collective-permute-done((bf16[128,2048]{1,0:T(8,128)(2,1)S(1)}, bf16[128,2048]{1,0:T(8,128)(2,1)S(1)}, u32[]{:S(2)}, u32[]{:S(2)}) %collective-permute-start.54) | collective-permute-done | bytes 524320 | tf_op jit(solution)/shard_map/ppermute | solution.py:449
  431.9 7.5 %collective-permute-done.57 = bf16[128,2048]{1,0:T(8,128)(2,1)S(1)} collective-permute-done((bf16[128,2048]{1,0:T(8,128)(2,1)S(1)}, bf16[128,2048]{1,0:T(8,128)(2,1)S(1)}, u32[]{:S(2)}, u32[]{:S(2)}) %collective-permute-start.57) | collective-permute-done | bytes 524320 | tf_op jit(solution)/shard_map/ppermute | solution.py:449
  451.8 6.6 %place_ffn.1 = (f32[2,704,2048]{2,1,0:T(8,128)}, f32[704,2048]{1,0:T(8,128)}) custom-call(s32[1]{0:T(128)} %bitcast.12.at.where.core, bf16[704,3072]{1,0:T(8,128)(2,1)S(1)} %copy-done.2, bf16[704,3072]{1,0:T(8,128)(2,1)S(1)} %copy-done.4), custom_call_target="tpu_custom_call" | custom-call | flops 8999999488 | bytes 27000000 | tf_op jit(solution)/shard_map/place_ffn/pallas_call | solution.py:635
  (410 shorter events, 248.1 us)
Async XLA Ops:
  7.2 113.1 %all-gather.4.cloned.1.call-start = ((), (), s32[]{:S(2)}) async-start(), calls=%async_computation.2 | async-start | bytes 5242880 | tf_op jit(solution)/shard_map/all_gather | solution.py:778
  12.0 15.1 %collective-permute-start.1 = (bf16[128,2048]{1,0:T(8,128)(2,1)S(1)}, bf16[128,2048]{1,0:T(8,128)(2,1)S(1)}, u32[]{:S(2)}, u32[]{:S(2)}) collective-permute-start(bf16[128,2048]{1,0:T(8,128)(2,1)S(1)} %fusion.6.refs_0_), channel_id=1, source_target_pairs={{0,2},{2,4},{4,6},{6,0},{1,3},{3,5},{5,7},{7,1},{8,10},{10,12},{12... | collective-permute-start | bytes 1572872 | tf_op jit(solution)/shard_map/ppermute | solution.py:441
  53.4 248.6 %reduce-scatter.3.cloned.1.call-start = ((), (), s32[]{:S(2)}) async-start(), calls=%async_computation.3 | async-start | bytes 5406720 | tf_op jit(solution)/shard_map/reduce_scatter | solution.py:766
  91.5 28.7 %collective-permute-start.12 = (bf16[128,2048]{1,0:T(8,128)(2,1)}, bf16[128,2048]{1,0:T(8,128)(2,1)S(1)}, u32[]{:S(2)}, u32[]{:S(2)}) collective-permute-start(bf16[128,2048]{1,0:T(8,128)(2,1)} %get-tuple-element.227), channel_id=1, source_target_pairs={{0,2},{2,4},{4,6},{6,0},{1,3},{3,5},{5,7},{7,1},{8,10},{10,12},{12... | collective-permute-start | bytes 1572872 | tf_op jit(solution)/shard_map/ppermute | solution.py:441
  104.6 15.7 %collective-permute-start.11 = (bf16[128,2048]{1,0:T(8,128)(2,1)S(1)}, bf16[128,2048]{1,0:T(8,128)(2,1)S(1)}, u32[]{:S(2)}, u32[]{:S(2)}) collective-permute-start(bf16[128,2048]{1,0:T(8,128)(2,1)S(1)} %pad_maximum_fusion.1), channel_id=1, source_target_pairs={{0,6},{2,0},{4,2},{6,4},{1,7},{3,1},{5,3},{7,5},{8,14},{10,8},{12,... | collective-permute-start | bytes 1572872 | tf_op jit(solution)/shard_map/ppermute | solution.py:445
  105.1 15.2 %collective-permute-start.13 = (bf16[128,2048]{1,0:T(8,128)(2,1)S(1)}, bf16[128,2048]{1,0:T(8,128)(2,1)}, u32[]{:S(2)}, u32[]{:S(2)}) collective-permute-start(bf16[128,2048]{1,0:T(8,128)(2,1)S(1)} %pad_maximum_fusion.2), channel_id=1, source_target_pairs={{0,1},{1,0},{2,3},{3,2},{4,5},{5,4},{6,7},{7,6},{8,9},{9,8},{10,11... | collective-permute-start | bytes 1572872 | tf_op jit(solution)/shard_map/ppermute | solution.py:449
  195.0 16.1 %collective-permute-start.25 = (bf16[64,2048]{1,0:T(8,128)(2,1)S(1)}, bf16[64,2048]{1,0:T(8,128)(2,1)S(1)}, u32[]{:S(2)}, u32[]{:S(2)}) collective-permute-start(bf16[64,2048]{1,0:T(8,128)(2,1)S(1)} %get-tuple-element.404), channel_id=1, source_target_pairs={{0,6},{2,0},{4,2},{6,4},{1,7},{3,1},{5,3},{7,5},{8,14},{10,8},{12,... | collective-permute-start | bytes 786440 | tf_op jit(solution)/shard_map/ppermute | solution.py:445
  211.2 24.6 %collective-permute-start.30 = (bf16[704,3072]{1,0:T(8,128)(2,1)}, bf16[704,3072]{1,0:T(8,128)(2,1)S(1)}, u32[]{:S(2)}, u32[]{:S(2)}) collective-permute-start(bf16[704,3072]{1,0:T(8,128)(2,1)} %ffn_grads.2), channel_id=1, source_target_pairs={{0,8},{8,0},{1,9},{9,1},{2,10},{10,2},{3,11},{11,3},{4,12},{12,4},... | collective-permute-start | bytes 12976136 | tf_op jit(solution)/shard_map/ppermute | solution.py:765
  219.1 15.3 %collective-permute-start.28 = (bf16[128,2048]{1,0:T(8,128)(2,1)S(1)}, bf16[128,2048]{1,0:T(8,128)(2,1)S(1)}, u32[]{:S(2)}, u32[]{:S(2)}) collective-permute-start(bf16[128,2048]{1,0:T(8,128)(2,1)S(1)} %copy-done.75), channel_id=1, source_target_pairs={{0,2},{2,4},{4,6},{6,0},{1,3},{3,5},{5,7},{7,1},{8,10},{10,12},{12... | collective-permute-start | bytes 1572872 | tf_op jit(solution)/shard_map/ppermute | solution.py:441
  219.3 15.1 %collective-permute-start.27 = (bf16[128,2048]{1,0:T(8,128)(2,1)S(1)}, bf16[128,2048]{1,0:T(8,128)(2,1)S(1)}, u32[]{:S(2)}, u32[]{:S(2)}) collective-permute-start(bf16[128,2048]{1,0:T(8,128)(2,1)S(1)} %pad_maximum_fusion.3), channel_id=1, source_target_pairs={{0,6},{2,0},{4,2},{6,4},{1,7},{3,1},{5,3},{7,5},{8,14},{10,8},{12,... | collective-permute-start | bytes 1572872 | tf_op jit(solution)/shard_map/ppermute | solution.py:445
  253.8 132.7 %all-gather.6.cloned.1.call-start = ((), (), s32[]{:S(2)}) async-start(), calls=%async_computation.4 | async-start | bytes 5406720 | tf_op jit(solution)/shard_map/all_gather | solution.py:812
  302.0 33.8 %collective-permute-start.42 = (bf16[176,3072]{1,0:T(8,128)(2,1)}, bf16[176,3072]{1,0:T(8,128)(2,1)}, u32[]{:S(2)}, u32[]{:S(2)}) collective-permute-start(bf16[176,3072]{1,0:T(8,128)(2,1)} %reduce-scatter.3.cloned.1.call-done), channel_id=1, source_target_pairs={{0,16},{16,0},{1,17},{17,1},{2,18},{18,2},{3,19},{19,3},{4,20},{20... | collective-permute-start | bytes 3244040 | tf_op jit(solution)/shard_map/ppermute | solution.py:733
  338.9 106.3 %reduce-scatter.5.cloned.1.call-start = ((), (), s32[]{:S(2)}) async-start(), calls=%async_computation.5 | async-start | bytes 3276800 | tf_op jit(solution)/shard_map/reduce_scatter | solution.py:766
  346.2 15.7 %collective-permute-start.43 = (bf16[1280,1024]{1,0:T(8,128)(2,1)S(1)}, bf16[1280,1024]{1,0:T(8,128)(2,1)S(1)}, u32[]{:S(2)}, u32[]{:S(2)}) collective-permute-start(bf16[1280,1024]{1,0:T(8,128)(2,1)S(1)} %mixer_grads.2), channel_id=1, source_target_pairs={{0,8},{8,0},{1,9},{9,1},{2,10},{10,2},{3,11},{11,3},{4,12},{12,4},... | collective-permute-start | bytes 7864328 | tf_op jit(solution)/shard_map/ppermute | solution.py:765
  348.0 27.4 %collective-permute-start.46 = (bf16[64,2048]{1,0:T(8,128)(2,1)}, bf16[64,2048]{1,0:T(8,128)(2,1)}, u32[]{:S(2)}, u32[]{:S(2)}) collective-permute-start(bf16[64,2048]{1,0:T(8,128)(2,1)} %get-tuple-element.400), channel_id=1, source_target_pairs={{0,6},{2,0},{4,2},{6,4},{1,7},{3,1},{5,3},{7,5},{8,14},{10,8},{12,... | collective-permute-start | bytes 786440 | tf_op jit(solution)/shard_map/ppermute | solution.py:445
  350.7 25.6 %collective-permute-start.47 = (bf16[64,2048]{1,0:T(8,128)(2,1)}, bf16[64,2048]{1,0:T(8,128)(2,1)}, u32[]{:S(2)}, u32[]{:S(2)}) collective-permute-start(bf16[64,2048]{1,0:T(8,128)(2,1)} %get-tuple-element.399), channel_id=1, source_target_pairs={{0,2},{2,4},{4,6},{6,0},{1,3},{3,5},{5,7},{7,1},{8,10},{10,12},{12... | collective-permute-start | bytes 786440 | tf_op jit(solution)/shard_map/ppermute | solution.py:441
  351.4 45.7 %collective-permute-start.52 = (bf16[128,2048]{1,0:T(8,128)(2,1)}, bf16[128,2048]{1,0:T(8,128)(2,1)}, u32[]{:S(2)}, u32[]{:S(2)}) collective-permute-start(bf16[128,2048]{1,0:T(8,128)(2,1)} %get-tuple-element.334), channel_id=1, source_target_pairs={{0,2},{2,4},{4,6},{6,0},{1,3},{3,5},{5,7},{7,1},{8,10},{10,12},{12... | collective-permute-start | bytes 1572872 | tf_op jit(solution)/shard_map/ppermute | solution.py:441
  375.4 22.2 %collective-permute-start.49 = (bf16[128,2048]{1,0:T(8,128)(2,1)}, bf16[128,2048]{1,0:T(8,128)(2,1)}, u32[]{:S(2)}, u32[]{:S(2)}) collective-permute-start(bf16[128,2048]{1,0:T(8,128)(2,1)} %copy-done.5), channel_id=1, source_target_pairs={{0,2},{2,4},{4,6},{6,0},{1,3},{3,5},{5,7},{7,1},{8,10},{10,12},{12... | collective-permute-start | bytes 1572872 | tf_op jit(solution)/shard_map/ppermute | solution.py:441
  386.5 112.0 %all-gather.8.cloned.1.call-start = ((), (), s32[]{:S(2)}) async-start(), calls=%async_computation.6 | async-start | bytes 3276800 | tf_op jit(solution)/shard_map/all_gather | solution.py:823
  393.7 49.4 %collective-permute-start.60 = (bf16[704,3072]{1,0:T(8,128)(2,1)}, bf16[704,3072]{1,0:T(8,128)(2,1)S(1)}, u32[]{:S(2)}, u32[]{:S(2)}) collective-permute-start(bf16[704,3072]{1,0:T(8,128)(2,1)} %all-gather.6.cloned.1.call-done.own_ref), channel_id=1, source_target_pairs={{0,8},{8,0},{1,9},{9,1},{2,10},{10,2},{3,11},{11,3},{4,12},{12,4},... | collective-permute-start | bytes 12976136 | tf_op jit(solution)/shard_map/ppermute | solution.py:765
  397.1 15.1 %collective-permute-start.51 = (bf16[128,2048]{1,0:T(8,128)(2,1)S(1)}, bf16[128,2048]{1,0:T(8,128)(2,1)S(1)}, u32[]{:S(2)}, u32[]{:S(2)}) collective-permute-start(bf16[128,2048]{1,0:T(8,128)(2,1)S(1)} %pad_maximum_fusion.7), channel_id=1, source_target_pairs={{0,6},{2,0},{4,2},{6,4},{1,7},{3,1},{5,3},{7,5},{8,14},{10,8},{12,... | collective-permute-start | bytes 1572872 | tf_op jit(solution)/shard_map/ppermute | solution.py:445
  397.7 18.6 %collective-permute-start.53 = (bf16[128,2048]{1,0:T(8,128)(2,1)S(1)}, bf16[128,2048]{1,0:T(8,128)(2,1)S(1)}, u32[]{:S(2)}, u32[]{:S(2)}) collective-permute-start(bf16[128,2048]{1,0:T(8,128)(2,1)S(1)} %pad_maximum_fusion.8), channel_id=1, source_target_pairs={{0,1},{1,0},{2,3},{3,2},{4,5},{5,4},{6,7},{7,6},{8,9},{9,8},{10,11... | collective-permute-start | bytes 1572872 | tf_op jit(solution)/shard_map/ppermute | solution.py:449
  420.7 18.7 %collective-permute-start.57 = (bf16[128,2048]{1,0:T(8,128)(2,1)S(1)}, bf16[128,2048]{1,0:T(8,128)(2,1)S(1)}, u32[]{:S(2)}, u32[]{:S(2)}) collective-permute-start(bf16[128,2048]{1,0:T(8,128)(2,1)S(1)} %add_convert_fusion.3), channel_id=1, source_target_pairs={{0,1},{1,0},{2,3},{3,2},{4,5},{5,4},{6,7},{7,6},{8,9},{9,8},{10,11... | collective-permute-start | bytes 1572872 | tf_op jit(solution)/shard_map/ppermute | solution.py:449
  445.2 15.6 %collective-permute-start.61 = (bf16[320,1024]{1,0:T(8,128)(2,1)}, bf16[320,1024]{1,0:T(8,128)(2,1)S(1)}, u32[]{:S(2)}, u32[]{:S(2)}) collective-permute-start(bf16[320,1024]{1,0:T(8,128)(2,1)} %reduce-scatter.5.cloned.1.call-done), channel_id=1, source_target_pairs={{0,16},{16,0},{1,17},{17,1},{2,18},{18,2},{3,19},{19,3},{4,20},{20... | collective-permute-start | bytes 1966088 | tf_op jit(solution)/shard_map/ppermute | solution.py:822
  (133 other events, 1591.6 us)
Sparse Core Ops, SparseCore 0:
  53.5 60.9 all-gather.3
  253.9 48.0 reduce-scatter.2
  339.0 47.4 all-gather.5
  389.3 34.3 reduce-scatter.4
  462.0 36.4 all-gather.7
